TPU v7x, 128 devices: a whole 4x4x4 slice. The times are simulated.
128 devices in a mesh: row: 16 (over z, y_hi, core), col: 8 (over x, y_lo).
Axes of the slice: x: 4, y: 4 (y_hi: 2, y_lo: 2; y = y_hi * 2 + y_lo), z: 4, core: 2. Of those that a mesh axis runs over, the one named last changes fastest.
Arguments:
- hamiltonian: bfloat16 [6144, 6144], P('row', 'col'), may hold values from -6 to 6, as said below
- density: bfloat16 [6144, 6144], P('row', 'col'), as said below
- h_pattern: int32 [96, 96], P('row', 'col'), may hold values from 0 to 1, as said below
- p_pattern: int32 [96, 96], P('row', 'col'), may hold values from 0 to 1, as said below
- keep_mask: int32 [96, 96], P('row', 'col'), may hold values from 0 to 1, as said below
Outputs:
- gradient: float32 [6144, 6144], P('row', 'col')
Inputs may be any that keep to these rules, and one draw needn't show every extreme that they name: `hamiltonian`: Symmetric. `density`: Symmetric. `h_pattern`: each entry is 0 or 1; symmetric; every diagonal entry is 1, and the share of ones falls with the distance between block indices. `p_pattern`: each entry is 0 or 1; symmetric; every diagonal entry is 1, and the share of ones falls with the distance between block indices. `keep_mask`: each entry is 0 or 1; symmetric; every diagonal entry is 1, and the share of ones falls with the distance between block indices.
All inputs are finite; a program needn't handle non-finite values.
Results may differ from a plain program's by a relative error of at most 0.0003.
Values may be sent and summed in bfloat16 or wider, within the bound.
A program may use at most 128 MiB of HBM per device.

v0:
```python
import jax
import jax.numpy as jnp
from jax import lax
from jax.sharding import PartitionSpec as P


def passed_along(value, axis, by):
    peers = lax.axis_size(axis)
    return lax.ppermute(value, axis, [(i, (i + by) % peers) for i in range(peers)])


def apply_blocks(matrix, pattern):
    block_rows, block_cols = pattern.shape
    block_width = matrix.shape[0] // block_rows
    blocks = matrix.reshape(block_rows, block_width, block_cols, block_width)
    blocks = blocks * pattern.astype(matrix.dtype)[:, None, :, None]
    return blocks.reshape(matrix.shape)


def split_tiles(matrix):
    tile_width = matrix.shape[0]
    return matrix.reshape(tile_width, 2, tile_width).transpose(1, 0, 2)


def multiply(left_side, right_side):
    return jnp.einsum("otik,otkj->otij", left_side, right_side, preferred_element_type=jnp.float32)


def west_one(stacked):
    arrived = passed_along(stacked[:, 0], "col", -1)
    return jnp.stack([stacked[:, 1], arrived], axis=1)


def north_one(stacked):
    return passed_along(stacked, "row", -1)


def cannon_plan(masked_ham_tile, masked_den_tile, keep_mask):
    masked_ham = split_tiles(masked_ham_tile)
    masked_den = split_tiles(masked_den_tile)
    left_side = jnp.stack([masked_ham, masked_den])
    right_side = jnp.stack([masked_den, masked_ham])
    grid_rows = lax.axis_size("row")
    bit_count = grid_rows.bit_length() - 1
    row_index = lax.axis_index("row")
    col_index = lax.axis_index("col")
    arrived = passed_along(left_side[:, 0], "col", -1)
    candidate = jnp.stack([left_side[:, 1], arrived], axis=1)
    left_side = jnp.where(row_index % 2 == 1, candidate, left_side)
    for bit_number in range(1, bit_count):
        candidate = passed_along(left_side, "col", -(1 << bit_number - 1))
        left_side = jnp.where((row_index >> bit_number) % 2 == 1, candidate, left_side)
    virtual = 2 * col_index + jnp.arange(2, dtype=jnp.int32)
    for bit_number in range(bit_count):
        candidate = passed_along(right_side, "row", -(1 << bit_number))
        chosen = ((virtual >> bit_number) % 2 == 1)[None, :, None, None]
        right_side = jnp.where(chosen, candidate, right_side)
    accumulated = jnp.zeros(left_side.shape, jnp.float32)

    def advance(turn_index, loop_state):
        running, left_now, right_now = loop_state
        running = running + multiply(left_now, right_now)
        return (running, west_one(left_now), north_one(right_now))

    accumulated, left_side, right_side = lax.fori_loop(
        0, grid_rows - 1, advance, (accumulated, left_side, right_side)
    )
    accumulated = accumulated + multiply(left_side, right_side)
    difference = accumulated[0] - accumulated[1]
    tile_width = difference.shape[1]
    joined = difference.transpose(1, 0, 2).reshape(tile_width, 2 * tile_width)
    return apply_blocks(joined, keep_mask)


def shards(hamiltonian, density, h_pattern, p_pattern, keep_mask):
    masked_ham_tile = apply_blocks(hamiltonian, h_pattern)
    masked_den_tile = apply_blocks(density, p_pattern)
    return cannon_plan(masked_ham_tile, masked_den_tile, keep_mask)


def solution(mesh):
    return jax.shard_map(
        shards,
        mesh=mesh,
        in_specs=(
            P("row", "col"),
            P("row", "col"),
            P("row", "col"),
            P("row", "col"),
            P("row", "col"),
        ),
        out_specs=P("row", "col"),
        check_vma=False,
    )
```

profile of v0, /device:TPU:1, one launch (start us, length us, event | category | flops | bytes accessed | tf_op | source)
XLA Modules:
  0.0 635.9 jit_solution(13467085827932519884)
XLA Ops:
  7.7 3.6 collective-permute-start.2
  11.3 7.5 %collective-permute-done.2 = bf16[2,384,384]{1,2,0:T(8,128)(2,1)} collective-permute-done((bf16[2,384,384]{1,2,0:T(8,128)(2,1)S(1)}, bf16[2,384,384]{1,2,0:T(8,128)(2,1)}, u32[]{:S(2)}, u32[]{:S(2)}) %collective-permute-start.2) | collective-permute-done | bytes 589856 | tf_op jit(solution)/shard_map/ppermute | solution.py:9
  18.7 17.5 %collective-permute-done.6 = bf16[2,2,384,384]{2,3,1,0:T(8,128)(2,1)} collective-permute-done((bf16[2,2,384,384]{2,3,1,0:T(8,128)(2,1)S(1)}, bf16[2,2,384,384]{2,3,1,0:T(8,128)(2,1)}, u32[]{:S(2)}, u32[]{:S(2)}) %collective-permute-start.6) | collective-permute-done | bytes 1179680 | tf_op jit(solution)/shard_map/ppermute | solution.py:9
  36.2 2.0 broadcast_select_fusion
  38.3 5.2 collective-permute-start.7
  43.5 50.0 %collective-permute-done.7 = bf16[2,2,384,384]{2,3,1,0:T(8,128)(2,1)} collective-permute-done((bf16[2,2,384,384]{2,3,1,0:T(8,128)(2,1)S(1)}, bf16[2,2,384,384]{2,3,1,0:T(8,128)(2,1)}, u32[]{:S(2)}, u32[]{:S(2)}) %collective-permute-start.7) | collective-permute-done | bytes 1179680 | tf_op jit(solution)/shard_map/ppermute | solution.py:9
  94.9 3.2 collective-permute-start.8
  98.3 2.8 collective-permute-start.4
  101.1 21.5 %collective-permute-done.8 = bf16[2,2,384,384]{2,3,1,0:T(8,128)(2,1)} collective-permute-done((bf16[2,2,384,384]{2,3,1,0:T(8,128)(2,1)S(1)}, bf16[2,2,384,384]{2,3,1,0:T(8,128)(2,1)}, u32[]{:S(2)}, u32[]{:S(2)}) %collective-permute-start.8) | collective-permute-done | bytes 1179680 | tf_op jit(solution)/shard_map/ppermute | solution.py:9
  122.6 2.5 broadcast_select_fusion.2
  125.1 3.3 collective-permute-start.9
  129.6 2.7 collective-permute-start.5
  132.6 1.7 mul.44
  134.3 19.1 %collective-permute-done.9 = bf16[2,2,384,384]{2,3,1,0:T(8,128)(2,1)} collective-permute-done((bf16[2,2,384,384]{2,3,1,0:T(8,128)(2,1)}, bf16[2,2,384,384]{2,3,1,0:T(8,128)(2,1)}, u32[]{:S(2)}, u32[]{:S(2)}) %collective-permute-start.9) | collective-permute-done | bytes 1179680 | tf_op jit(solution)/shard_map/ppermute | solution.py:9
  153.4 1.8 broadcast_select_fusion.3
  159.6 469.5 %while.15 = (s32[]{:T(128)}, f32[2,2,384,384]{3,2,1,0:T(8,128)}, bf16[2,2,384,384]{3,2,0,1:T(8,128)(2,1)S(1)}, bf16[2,2,384,384]{3,2,1,0:T(8,128)(2,1)}, s32[]{:T(128)}, /*index=5*/s32[]{:T(128)}) while((s32[]{:T(128)}, f32[2,2,384,384]{3,2,1,0:T(8,128)}, bf16[2,2,384,384]{3,2,0,1:T(8,128)(2,1)S(1)}, ...), condition=%wide.region_1.2_spmd.clone, body=%wide.region_0.1_spmd.clone.sunk | while | flops 454754304 | bytes 21233824 | solution.py:65
  160.9 2.4 collective-permute-start.1
  164.2 2.3 select_add_fusion.2
  166.5 10.1 %collective-permute-done = bf16[2,384,384]{2,1,0:T(8,128)(2,1)S(1)} collective-permute-done((bf16[2,384,384]{2,1,0:T(8,128)(2,1)}, bf16[2,384,384]{2,1,0:T(8,128)(2,1)S(1)}, u32[]{:S(2)}, u32[]{:S(2)}) %collective-permute-start) | collective-permute-done | bytes 589856 | tf_op jit(solution)/shard_map/while/body/eval_jaxpr/ppermute | solution.py:9
  176.8 16.5 %collective-permute-done.1 = bf16[2,2,384,384]{3,2,1,0:T(8,128)(2,1)} collective-permute-done((bf16[2,2,384,384]{3,2,1,0:T(8,128)(2,1)S(1)}, bf16[2,2,384,384]{3,2,1,0:T(8,128)(2,1)}, u32[]{:S(2)}, u32[]{:S(2)}) %collective-permute-start.1) | collective-permute-done | bytes 1179680 | tf_op jit(solution)/shard_map/while/body/eval_jaxpr/ppermute | solution.py:9
  195.6 4.0 select_add_fusion.2
  199.5 10.9 %collective-permute-done = bf16[2,384,384]{2,1,0:T(8,128)(2,1)S(1)} collective-permute-done((bf16[2,384,384]{2,1,0:T(8,128)(2,1)}, bf16[2,384,384]{2,1,0:T(8,128)(2,1)S(1)}, u32[]{:S(2)}, u32[]{:S(2)}) %collective-permute-start) | collective-permute-done | bytes 589856 | tf_op jit(solution)/shard_map/while/body/eval_jaxpr/ppermute | solution.py:9
  210.5 14.0 %collective-permute-done.1 = bf16[2,2,384,384]{3,2,1,0:T(8,128)(2,1)} collective-permute-done((bf16[2,2,384,384]{3,2,1,0:T(8,128)(2,1)S(1)}, bf16[2,2,384,384]{3,2,1,0:T(8,128)(2,1)}, u32[]{:S(2)}, u32[]{:S(2)}) %collective-permute-start.1) | collective-permute-done | bytes 1179680 | tf_op jit(solution)/shard_map/while/body/eval_jaxpr/ppermute | solution.py:9
  226.7 4.0 select_add_fusion.2
  230.7 7.5 %collective-permute-done = bf16[2,384,384]{2,1,0:T(8,128)(2,1)S(1)} collective-permute-done((bf16[2,384,384]{2,1,0:T(8,128)(2,1)}, bf16[2,384,384]{2,1,0:T(8,128)(2,1)S(1)}, u32[]{:S(2)}, u32[]{:S(2)}) %collective-permute-start) | collective-permute-done | bytes 589856 | tf_op jit(solution)/shard_map/while/body/eval_jaxpr/ppermute | solution.py:9
  238.3 17.3 %collective-permute-done.1 = bf16[2,2,384,384]{3,2,1,0:T(8,128)(2,1)} collective-permute-done((bf16[2,2,384,384]{3,2,1,0:T(8,128)(2,1)S(1)}, bf16[2,2,384,384]{3,2,1,0:T(8,128)(2,1)}, u32[]{:S(2)}, u32[]{:S(2)}) %collective-permute-start.1) | collective-permute-done | bytes 1179680 | tf_op jit(solution)/shard_map/while/body/eval_jaxpr/ppermute | solution.py:9
  257.9 4.0 select_add_fusion.2
  261.8 8.2 %collective-permute-done = bf16[2,384,384]{2,1,0:T(8,128)(2,1)S(1)} collective-permute-done((bf16[2,384,384]{2,1,0:T(8,128)(2,1)}, bf16[2,384,384]{2,1,0:T(8,128)(2,1)S(1)}, u32[]{:S(2)}, u32[]{:S(2)}) %collective-permute-start) | collective-permute-done | bytes 589856 | tf_op jit(solution)/shard_map/while/body/eval_jaxpr/ppermute | solution.py:9
  270.2 16.5 %collective-permute-done.1 = bf16[2,2,384,384]{3,2,1,0:T(8,128)(2,1)} collective-permute-done((bf16[2,2,384,384]{3,2,1,0:T(8,128)(2,1)S(1)}, bf16[2,2,384,384]{3,2,1,0:T(8,128)(2,1)}, u32[]{:S(2)}, u32[]{:S(2)}) %collective-permute-start.1) | collective-permute-done | bytes 1179680 | tf_op jit(solution)/shard_map/while/body/eval_jaxpr/ppermute | solution.py:9
  288.9 4.0 select_add_fusion.2
  292.8 6.9 %collective-permute-done = bf16[2,384,384]{2,1,0:T(8,128)(2,1)S(1)} collective-permute-done((bf16[2,384,384]{2,1,0:T(8,128)(2,1)}, bf16[2,384,384]{2,1,0:T(8,128)(2,1)S(1)}, u32[]{:S(2)}, u32[]{:S(2)}) %collective-permute-start) | collective-permute-done | bytes 589856 | tf_op jit(solution)/shard_map/while/body/eval_jaxpr/ppermute | solution.py:9
  299.9 17.9 %collective-permute-done.1 = bf16[2,2,384,384]{3,2,1,0:T(8,128)(2,1)} collective-permute-done((bf16[2,2,384,384]{3,2,1,0:T(8,128)(2,1)S(1)}, bf16[2,2,384,384]{3,2,1,0:T(8,128)(2,1)}, u32[]{:S(2)}, u32[]{:S(2)}) %collective-permute-start.1) | collective-permute-done | bytes 1179680 | tf_op jit(solution)/shard_map/while/body/eval_jaxpr/ppermute | solution.py:9
  320.0 4.0 select_add_fusion.2
  324.0 7.0 %collective-permute-done = bf16[2,384,384]{2,1,0:T(8,128)(2,1)S(1)} collective-permute-done((bf16[2,384,384]{2,1,0:T(8,128)(2,1)}, bf16[2,384,384]{2,1,0:T(8,128)(2,1)S(1)}, u32[]{:S(2)}, u32[]{:S(2)}) %collective-permute-start) | collective-permute-done | bytes 589856 | tf_op jit(solution)/shard_map/while/body/eval_jaxpr/ppermute | solution.py:9
  331.2 17.8 %collective-permute-done.1 = bf16[2,2,384,384]{3,2,1,0:T(8,128)(2,1)} collective-permute-done((bf16[2,2,384,384]{3,2,1,0:T(8,128)(2,1)S(1)}, bf16[2,2,384,384]{3,2,1,0:T(8,128)(2,1)}, u32[]{:S(2)}, u32[]{:S(2)}) %collective-permute-start.1) | collective-permute-done | bytes 1179680 | tf_op jit(solution)/shard_map/while/body/eval_jaxpr/ppermute | solution.py:9
  351.2 4.0 select_add_fusion.2
  355.1 7.1 %collective-permute-done = bf16[2,384,384]{2,1,0:T(8,128)(2,1)S(1)} collective-permute-done((bf16[2,384,384]{2,1,0:T(8,128)(2,1)}, bf16[2,384,384]{2,1,0:T(8,128)(2,1)S(1)}, u32[]{:S(2)}, u32[]{:S(2)}) %collective-permute-start) | collective-permute-done | bytes 589856 | tf_op jit(solution)/shard_map/while/body/eval_jaxpr/ppermute | solution.py:9
  362.3 17.6 %collective-permute-done.1 = bf16[2,2,384,384]{3,2,1,0:T(8,128)(2,1)} collective-permute-done((bf16[2,2,384,384]{3,2,1,0:T(8,128)(2,1)S(1)}, bf16[2,2,384,384]{3,2,1,0:T(8,128)(2,1)}, u32[]{:S(2)}, u32[]{:S(2)}) %collective-permute-start.1) | collective-permute-done | bytes 1179680 | tf_op jit(solution)/shard_map/while/body/eval_jaxpr/ppermute | solution.py:9
  382.1 4.0 select_add_fusion.2
  386.1 6.9 %collective-permute-done = bf16[2,384,384]{2,1,0:T(8,128)(2,1)S(1)} collective-permute-done((bf16[2,384,384]{2,1,0:T(8,128)(2,1)}, bf16[2,384,384]{2,1,0:T(8,128)(2,1)S(1)}, u32[]{:S(2)}, u32[]{:S(2)}) %collective-permute-start) | collective-permute-done | bytes 589856 | tf_op jit(solution)/shard_map/while/body/eval_jaxpr/ppermute | solution.py:9
  393.1 17.9 %collective-permute-done.1 = bf16[2,2,384,384]{3,2,1,0:T(8,128)(2,1)} collective-permute-done((bf16[2,2,384,384]{3,2,1,0:T(8,128)(2,1)S(1)}, bf16[2,2,384,384]{3,2,1,0:T(8,128)(2,1)}, u32[]{:S(2)}, u32[]{:S(2)}) %collective-permute-start.1) | collective-permute-done | bytes 1179680 | tf_op jit(solution)/shard_map/while/body/eval_jaxpr/ppermute | solution.py:9
  413.3 4.0 select_add_fusion.2
  417.3 6.9 %collective-permute-done = bf16[2,384,384]{2,1,0:T(8,128)(2,1)S(1)} collective-permute-done((bf16[2,384,384]{2,1,0:T(8,128)(2,1)}, bf16[2,384,384]{2,1,0:T(8,128)(2,1)S(1)}, u32[]{:S(2)}, u32[]{:S(2)}) %collective-permute-start) | collective-permute-done | bytes 589856 | tf_op jit(solution)/shard_map/while/body/eval_jaxpr/ppermute | solution.py:9
  424.3 17.9 %collective-permute-done.1 = bf16[2,2,384,384]{3,2,1,0:T(8,128)(2,1)} collective-permute-done((bf16[2,2,384,384]{3,2,1,0:T(8,128)(2,1)S(1)}, bf16[2,2,384,384]{3,2,1,0:T(8,128)(2,1)}, u32[]{:S(2)}, u32[]{:S(2)}) %collective-permute-start.1) | collective-permute-done | bytes 1179680 | tf_op jit(solution)/shard_map/while/body/eval_jaxpr/ppermute | solution.py:9
  444.4 4.0 select_add_fusion.2
  448.4 6.9 %collective-permute-done = bf16[2,384,384]{2,1,0:T(8,128)(2,1)S(1)} collective-permute-done((bf16[2,384,384]{2,1,0:T(8,128)(2,1)}, bf16[2,384,384]{2,1,0:T(8,128)(2,1)S(1)}, u32[]{:S(2)}, u32[]{:S(2)}) %collective-permute-start) | collective-permute-done | bytes 589856 | tf_op jit(solution)/shard_map/while/body/eval_jaxpr/ppermute | solution.py:9
  455.5 17.9 %collective-permute-done.1 = bf16[2,2,384,384]{3,2,1,0:T(8,128)(2,1)} collective-permute-done((bf16[2,2,384,384]{3,2,1,0:T(8,128)(2,1)S(1)}, bf16[2,2,384,384]{3,2,1,0:T(8,128)(2,1)}, u32[]{:S(2)}, u32[]{:S(2)}) %collective-permute-start.1) | collective-permute-done | bytes 1179680 | tf_op jit(solution)/shard_map/while/body/eval_jaxpr/ppermute | solution.py:9
  475.6 4.0 select_add_fusion.2
  479.6 6.9 %collective-permute-done = bf16[2,384,384]{2,1,0:T(8,128)(2,1)S(1)} collective-permute-done((bf16[2,384,384]{2,1,0:T(8,128)(2,1)}, bf16[2,384,384]{2,1,0:T(8,128)(2,1)S(1)}, u32[]{:S(2)}, u32[]{:S(2)}) %collective-permute-start) | collective-permute-done | bytes 589856 | tf_op jit(solution)/shard_map/while/body/eval_jaxpr/ppermute | solution.py:9
  486.7 17.9 %collective-permute-done.1 = bf16[2,2,384,384]{3,2,1,0:T(8,128)(2,1)} collective-permute-done((bf16[2,2,384,384]{3,2,1,0:T(8,128)(2,1)S(1)}, bf16[2,2,384,384]{3,2,1,0:T(8,128)(2,1)}, u32[]{:S(2)}, u32[]{:S(2)}) %collective-permute-start.1) | collective-permute-done | bytes 1179680 | tf_op jit(solution)/shard_map/while/body/eval_jaxpr/ppermute | solution.py:9
  506.7 4.0 select_add_fusion.2
  510.7 6.9 %collective-permute-done = bf16[2,384,384]{2,1,0:T(8,128)(2,1)S(1)} collective-permute-done((bf16[2,384,384]{2,1,0:T(8,128)(2,1)}, bf16[2,384,384]{2,1,0:T(8,128)(2,1)S(1)}, u32[]{:S(2)}, u32[]{:S(2)}) %collective-permute-start) | collective-permute-done | bytes 589856 | tf_op jit(solution)/shard_map/while/body/eval_jaxpr/ppermute | solution.py:9
  517.8 17.9 %collective-permute-done.1 = bf16[2,2,384,384]{3,2,1,0:T(8,128)(2,1)} collective-permute-done((bf16[2,2,384,384]{3,2,1,0:T(8,128)(2,1)S(1)}, bf16[2,2,384,384]{3,2,1,0:T(8,128)(2,1)}, u32[]{:S(2)}, u32[]{:S(2)}) %collective-permute-start.1) | collective-permute-done | bytes 1179680 | tf_op jit(solution)/shard_map/while/body/eval_jaxpr/ppermute | solution.py:9
  537.9 4.0 select_add_fusion.2
  541.9 6.9 %collective-permute-done = bf16[2,384,384]{2,1,0:T(8,128)(2,1)S(1)} collective-permute-done((bf16[2,384,384]{2,1,0:T(8,128)(2,1)}, bf16[2,384,384]{2,1,0:T(8,128)(2,1)S(1)}, u32[]{:S(2)}, u32[]{:S(2)}) %collective-permute-start) | collective-permute-done | bytes 589856 | tf_op jit(solution)/shard_map/while/body/eval_jaxpr/ppermute | solution.py:9
  549.0 17.9 %collective-permute-done.1 = bf16[2,2,384,384]{3,2,1,0:T(8,128)(2,1)} collective-permute-done((bf16[2,2,384,384]{3,2,1,0:T(8,128)(2,1)S(1)}, bf16[2,2,384,384]{3,2,1,0:T(8,128)(2,1)}, u32[]{:S(2)}, u32[]{:S(2)}) %collective-permute-start.1) | collective-permute-done | bytes 1179680 | tf_op jit(solution)/shard_map/while/body/eval_jaxpr/ppermute | solution.py:9
  569.0 4.0 select_add_fusion.2
  573.0 6.9 %collective-permute-done = bf16[2,384,384]{2,1,0:T(8,128)(2,1)S(1)} collective-permute-done((bf16[2,384,384]{2,1,0:T(8,128)(2,1)}, bf16[2,384,384]{2,1,0:T(8,128)(2,1)S(1)}, u32[]{:S(2)}, u32[]{:S(2)}) %collective-permute-start) | collective-permute-done | bytes 589856 | tf_op jit(solution)/shard_map/while/body/eval_jaxpr/ppermute | solution.py:9
  580.1 17.9 %collective-permute-done.1 = bf16[2,2,384,384]{3,2,1,0:T(8,128)(2,1)} collective-permute-done((bf16[2,2,384,384]{3,2,1,0:T(8,128)(2,1)S(1)}, bf16[2,2,384,384]{3,2,1,0:T(8,128)(2,1)}, u32[]{:S(2)}, u32[]{:S(2)}) %collective-permute-start.1) | collective-permute-done | bytes 1179680 | tf_op jit(solution)/shard_map/while/body/eval_jaxpr/ppermute | solution.py:9
  600.2 4.0 select_add_fusion.2
  604.2 6.9 %collective-permute-done = bf16[2,384,384]{2,1,0:T(8,128)(2,1)S(1)} collective-permute-done((bf16[2,384,384]{2,1,0:T(8,128)(2,1)}, bf16[2,384,384]{2,1,0:T(8,128)(2,1)S(1)}, u32[]{:S(2)}, u32[]{:S(2)}) %collective-permute-start) | collective-permute-done | bytes 589856 | tf_op jit(solution)/shard_map/while/body/eval_jaxpr/ppermute | solution.py:9
  611.3 17.9 %collective-permute-done.1 = bf16[2,2,384,384]{3,2,1,0:T(8,128)(2,1)} collective-permute-done((bf16[2,2,384,384]{3,2,1,0:T(8,128)(2,1)S(1)}, bf16[2,2,384,384]{3,2,1,0:T(8,128)(2,1)}, u32[]{:S(2)}, u32[]{:S(2)}) %collective-permute-start.1) | collective-permute-done | bytes 1179680 | tf_op jit(solution)/shard_map/while/body/eval_jaxpr/ppermute | solution.py:9
  629.1 2.0 copy.23
  631.1 2.2 convolution_add_fusion
  (118 shorter events, 52.8 us)
Async XLA Ops:
  1.1 1.0 copy-start.3
  2.5 1.1 copy-start.1
  3.6 1.1 copy-start.2
  5.2 31.0 %collective-permute-start.6 = (bf16[2,2,384,384]{2,3,1,0:T(8,128)(2,1)S(1)}, bf16[2,2,384,384]{2,3,1,0:T(8,128)(2,1)}, u32[]{:S(2)}, u32[]{:S(2)}) collective-permute-start(bf16[2,2,384,384]{2,3,1,0:T(8,128)(2,1)S(1)} %pad_maximum_fusion.2), channel_id=1, source_target_pairs={{0,120},{8,0},{16,8},{24,16},{32,24},{40,32},{48,40},{56,48},{64,5... | collective-permute-start | bytes 3538952 | tf_op jit(solution)/shard_map/ppermute | solution.py:9
  7.7 11.1 %collective-permute-start.2 = (bf16[2,384,384]{1,2,0:T(8,128)(2,1)S(1)}, bf16[2,384,384]{1,2,0:T(8,128)(2,1)}, u32[]{:S(2)}, u32[]{:S(2)}) collective-permute-start(bf16[2,384,384]{1,2,0:T(8,128)(2,1)S(1)} %get-tuple-element.68), channel_id=1, source_target_pairs={{0,7},{1,0},{2,1},{3,2},{4,3},{5,4},{6,5},{7,6},{8,15},{9,8},{10,9... | collective-permute-start | bytes 1769480 | tf_op jit(solution)/shard_map/ppermute | solution.py:9
  38.3 55.2 %collective-permute-start.7 = (bf16[2,2,384,384]{2,3,1,0:T(8,128)(2,1)S(1)}, bf16[2,2,384,384]{2,3,1,0:T(8,128)(2,1)}, u32[]{:S(2)}, u32[]{:S(2)}) collective-permute-start(bf16[2,2,384,384]{2,3,1,0:T(8,128)(2,1)S(1)} %get-tuple-element.65), channel_id=1, source_target_pairs={{0,112},{8,120},{16,0},{24,8},{32,16},{40,24},{48,32},{56,40},{64,... | collective-permute-start | bytes 3538952 | tf_op jit(solution)/shard_map/ppermute | solution.py:9
  43.5 54.7 %collective-permute-start.3 = (bf16[2,2,384,384]{2,3,1,0:T(8,128)(2,1)S(1)}, bf16[2,2,384,384]{2,3,1,0:T(8,128)(2,1)}, u32[]{:S(2)}, u32[]{:S(2)}) collective-permute-start(bf16[2,2,384,384]{2,3,1,0:T(8,128)(2,1)S(1)} %get-tuple-element.66), channel_id=1, source_target_pairs={{0,7},{1,0},{2,1},{3,2},{4,3},{5,4},{6,5},{7,6},{8,15},{9,8},{10,9... | collective-permute-start | bytes 3538952 | tf_op jit(solution)/shard_map/ppermute | solution.py:9
  94.9 27.7 %collective-permute-start.8 = (bf16[2,2,384,384]{2,3,1,0:T(8,128)(2,1)S(1)}, bf16[2,2,384,384]{2,3,1,0:T(8,128)(2,1)}, u32[]{:S(2)}, u32[]{:S(2)}) collective-permute-start(bf16[2,2,384,384]{2,3,1,0:T(8,128)(2,1)S(1)} %broadcast_select_fusion.1), channel_id=1, source_target_pairs={{0,96},{8,104},{16,112},{24,120},{32,0},{40,8},{48,16},{56,24},{64... | collective-permute-start | bytes 3538952 | tf_op jit(solution)/shard_map/ppermute | solution.py:9
  98.3 30.2 %collective-permute-start.4 = (bf16[2,2,384,384]{2,3,1,0:T(8,128)(2,1)S(1)}, bf16[2,2,384,384]{2,3,1,0:T(8,128)(2,1)S(1)}, u32[]{:S(2)}, u32[]{:S(2)}) collective-permute-start(bf16[2,2,384,384]{2,3,1,0:T(8,128)(2,1)S(1)} %broadcast_select_fusion.4), channel_id=1, source_target_pairs={{0,6},{1,7},{2,0},{3,1},{4,2},{5,3},{6,4},{7,5},{8,14},{9,15},{10,... | collective-permute-start | bytes 3538952 | tf_op jit(solution)/shard_map/ppermute | solution.py:9
  125.1 28.3 %collective-permute-start.9 = (bf16[2,2,384,384]{2,3,1,0:T(8,128)(2,1)}, bf16[2,2,384,384]{2,3,1,0:T(8,128)(2,1)}, u32[]{:S(2)}, u32[]{:S(2)}) collective-permute-start(bf16[2,2,384,384]{2,3,1,0:T(8,128)(2,1)} %broadcast_select_fusion.2), channel_id=1, source_target_pairs={{0,64},{8,72},{16,80},{24,88},{32,96},{40,104},{48,112},{56,120},{... | collective-permute-start | bytes 3538952 | tf_op jit(solution)/shard_map/ppermute | solution.py:9
  128.4 3.9 copy-start.4
  129.6 27.8 %collective-permute-start.5 = (bf16[2,2,384,384]{2,3,1,0:T(8,128)(2,1)}, bf16[2,2,384,384]{2,3,1,0:T(8,128)(2,1)}, u32[]{:S(2)}, u32[]{:S(2)}) collective-permute-start(bf16[2,2,384,384]{2,3,1,0:T(8,128)(2,1)} %broadcast_select_fusion.5), channel_id=1, source_target_pairs={{0,4},{1,5},{2,6},{3,7},{4,0},{5,1},{6,2},{7,3},{8,12},{9,13},{10,... | collective-permute-start | bytes 3538952 | tf_op jit(solution)/shard_map/ppermute | solution.py:9
  160.9 32.5 %collective-permute-start.1 = (bf16[2,2,384,384]{3,2,1,0:T(8,128)(2,1)S(1)}, bf16[2,2,384,384]{3,2,1,0:T(8,128)(2,1)}, u32[]{:S(2)}, u32[]{:S(2)}) collective-permute-start(bf16[2,2,384,384]{3,2,1,0:T(8,128)(2,1)S(1)} %copy.40), channel_id=1, source_target_pairs={{0,120},{8,0},{16,8},{24,16},{32,24},{40,32},{48,40},{56,48},{64,5... | collective-permute-start | bytes 3538952 | tf_op jit(solution)/shard_map/while/body/eval_jaxpr/ppermute | solution.py:9
  164.2 12.4 %collective-permute-start = (bf16[2,384,384]{2,1,0:T(8,128)(2,1)}, bf16[2,384,384]{2,1,0:T(8,128)(2,1)S(1)}, u32[]{:S(2)}, u32[]{:S(2)}) collective-permute-start(bf16[2,384,384]{2,1,0:T(8,128)(2,1)} %get-tuple-element.98), channel_id=1, source_target_pairs={{0,7},{1,0},{2,1},{3,2},{4,3},{5,4},{6,5},{7,6},{8,15},{9,8},{10,9... | collective-permute-start | bytes 1769480 | tf_op jit(solution)/shard_map/while/body/eval_jaxpr/ppermute | solution.py:9
  194.6 29.9 %collective-permute-start.1 = (bf16[2,2,384,384]{3,2,1,0:T(8,128)(2,1)S(1)}, bf16[2,2,384,384]{3,2,1,0:T(8,128)(2,1)}, u32[]{:S(2)}, u32[]{:S(2)}) collective-permute-start(bf16[2,2,384,384]{3,2,1,0:T(8,128)(2,1)S(1)} %copy.40), channel_id=1, source_target_pairs={{0,120},{8,0},{16,8},{24,16},{32,24},{40,32},{48,40},{56,48},{64,5... | collective-permute-start | bytes 3538952 | tf_op jit(solution)/shard_map/while/body/eval_jaxpr/ppermute | solution.py:9
  195.6 14.8 %collective-permute-start = (bf16[2,384,384]{2,1,0:T(8,128)(2,1)}, bf16[2,384,384]{2,1,0:T(8,128)(2,1)S(1)}, u32[]{:S(2)}, u32[]{:S(2)}) collective-permute-start(bf16[2,384,384]{2,1,0:T(8,128)(2,1)} %get-tuple-element.98), channel_id=1, source_target_pairs={{0,7},{1,0},{2,1},{3,2},{4,3},{5,4},{6,5},{7,6},{8,15},{9,8},{10,9... | collective-permute-start | bytes 1769480 | tf_op jit(solution)/shard_map/while/body/eval_jaxpr/ppermute | solution.py:9
  225.8 29.9 %collective-permute-start.1 = (bf16[2,2,384,384]{3,2,1,0:T(8,128)(2,1)S(1)}, bf16[2,2,384,384]{3,2,1,0:T(8,128)(2,1)}, u32[]{:S(2)}, u32[]{:S(2)}) collective-permute-start(bf16[2,2,384,384]{3,2,1,0:T(8,128)(2,1)S(1)} %copy.40), channel_id=1, source_target_pairs={{0,120},{8,0},{16,8},{24,16},{32,24},{40,32},{48,40},{56,48},{64,5... | collective-permute-start | bytes 3538952 | tf_op jit(solution)/shard_map/while/body/eval_jaxpr/ppermute | solution.py:9
  226.7 11.5 %collective-permute-start = (bf16[2,384,384]{2,1,0:T(8,128)(2,1)}, bf16[2,384,384]{2,1,0:T(8,128)(2,1)S(1)}, u32[]{:S(2)}, u32[]{:S(2)}) collective-permute-start(bf16[2,384,384]{2,1,0:T(8,128)(2,1)} %get-tuple-element.98), channel_id=1, source_target_pairs={{0,7},{1,0},{2,1},{3,2},{4,3},{5,4},{6,5},{7,6},{8,15},{9,8},{10,9... | collective-permute-start | bytes 1769480 | tf_op jit(solution)/shard_map/while/body/eval_jaxpr/ppermute | solution.py:9
  256.9 29.7 %collective-permute-start.1 = (bf16[2,2,384,384]{3,2,1,0:T(8,128)(2,1)S(1)}, bf16[2,2,384,384]{3,2,1,0:T(8,128)(2,1)}, u32[]{:S(2)}, u32[]{:S(2)}) collective-permute-start(bf16[2,2,384,384]{3,2,1,0:T(8,128)(2,1)S(1)} %copy.40), channel_id=1, source_target_pairs={{0,120},{8,0},{16,8},{24,16},{32,24},{40,32},{48,40},{56,48},{64,5... | collective-permute-start | bytes 3538952 | tf_op jit(solution)/shard_map/while/body/eval_jaxpr/ppermute | solution.py:9
  257.9 12.2 %collective-permute-start = (bf16[2,384,384]{2,1,0:T(8,128)(2,1)}, bf16[2,384,384]{2,1,0:T(8,128)(2,1)S(1)}, u32[]{:S(2)}, u32[]{:S(2)}) collective-permute-start(bf16[2,384,384]{2,1,0:T(8,128)(2,1)} %get-tuple-element.98), channel_id=1, source_target_pairs={{0,7},{1,0},{2,1},{3,2},{4,3},{5,4},{6,5},{7,6},{8,15},{9,8},{10,9... | collective-permute-start | bytes 1769480 | tf_op jit(solution)/shard_map/while/body/eval_jaxpr/ppermute | solution.py:9
  287.9 29.9 %collective-permute-start.1 = (bf16[2,2,384,384]{3,2,1,0:T(8,128)(2,1)S(1)}, bf16[2,2,384,384]{3,2,1,0:T(8,128)(2,1)}, u32[]{:S(2)}, u32[]{:S(2)}) collective-permute-start(bf16[2,2,384,384]{3,2,1,0:T(8,128)(2,1)S(1)} %copy.40), channel_id=1, source_target_pairs={{0,120},{8,0},{16,8},{24,16},{32,24},{40,32},{48,40},{56,48},{64,5... | collective-permute-start | bytes 3538952 | tf_op jit(solution)/shard_map/while/body/eval_jaxpr/ppermute | solution.py:9
  288.9 10.9 %collective-permute-start = (bf16[2,384,384]{2,1,0:T(8,128)(2,1)}, bf16[2,384,384]{2,1,0:T(8,128)(2,1)S(1)}, u32[]{:S(2)}, u32[]{:S(2)}) collective-permute-start(bf16[2,384,384]{2,1,0:T(8,128)(2,1)} %get-tuple-element.98), channel_id=1, source_target_pairs={{0,7},{1,0},{2,1},{3,2},{4,3},{5,4},{6,5},{7,6},{8,15},{9,8},{10,9... | collective-permute-start | bytes 1769480 | tf_op jit(solution)/shard_map/while/body/eval_jaxpr/ppermute | solution.py:9
  319.1 29.9 %collective-permute-start.1 = (bf16[2,2,384,384]{3,2,1,0:T(8,128)(2,1)S(1)}, bf16[2,2,384,384]{3,2,1,0:T(8,128)(2,1)}, u32[]{:S(2)}, u32[]{:S(2)}) collective-permute-start(bf16[2,2,384,384]{3,2,1,0:T(8,128)(2,1)S(1)} %copy.40), channel_id=1, source_target_pairs={{0,120},{8,0},{16,8},{24,16},{32,24},{40,32},{48,40},{56,48},{64,5... | collective-permute-start | bytes 3538952 | tf_op jit(solution)/shard_map/while/body/eval_jaxpr/ppermute | solution.py:9
  320.0 11.0 %collective-permute-start = (bf16[2,384,384]{2,1,0:T(8,128)(2,1)}, bf16[2,384,384]{2,1,0:T(8,128)(2,1)S(1)}, u32[]{:S(2)}, u32[]{:S(2)}) collective-permute-start(bf16[2,384,384]{2,1,0:T(8,128)(2,1)} %get-tuple-element.98), channel_id=1, source_target_pairs={{0,7},{1,0},{2,1},{3,2},{4,3},{5,4},{6,5},{7,6},{8,15},{9,8},{10,9... | collective-permute-start | bytes 1769480 | tf_op jit(solution)/shard_map/while/body/eval_jaxpr/ppermute | solution.py:9
  350.2 29.7 %collective-permute-start.1 = (bf16[2,2,384,384]{3,2,1,0:T(8,128)(2,1)S(1)}, bf16[2,2,384,384]{3,2,1,0:T(8,128)(2,1)}, u32[]{:S(2)}, u32[]{:S(2)}) collective-permute-start(bf16[2,2,384,384]{3,2,1,0:T(8,128)(2,1)S(1)} %copy.40), channel_id=1, source_target_pairs={{0,120},{8,0},{16,8},{24,16},{32,24},{40,32},{48,40},{56,48},{64,5... | collective-permute-start | bytes 3538952 | tf_op jit(solution)/shard_map/while/body/eval_jaxpr/ppermute | solution.py:9
  351.2 11.0 %collective-permute-start = (bf16[2,384,384]{2,1,0:T(8,128)(2,1)}, bf16[2,384,384]{2,1,0:T(8,128)(2,1)S(1)}, u32[]{:S(2)}, u32[]{:S(2)}) collective-permute-start(bf16[2,384,384]{2,1,0:T(8,128)(2,1)} %get-tuple-element.98), channel_id=1, source_target_pairs={{0,7},{1,0},{2,1},{3,2},{4,3},{5,4},{6,5},{7,6},{8,15},{9,8},{10,9... | collective-permute-start | bytes 1769480 | tf_op jit(solution)/shard_map/while/body/eval_jaxpr/ppermute | solution.py:9
  381.2 29.9 %collective-permute-start.1 = (bf16[2,2,384,384]{3,2,1,0:T(8,128)(2,1)S(1)}, bf16[2,2,384,384]{3,2,1,0:T(8,128)(2,1)}, u32[]{:S(2)}, u32[]{:S(2)}) collective-permute-start(bf16[2,2,384,384]{3,2,1,0:T(8,128)(2,1)S(1)} %copy.40), channel_id=1, source_target_pairs={{0,120},{8,0},{16,8},{24,16},{32,24},{40,32},{48,40},{56,48},{64,5... | collective-permute-start | bytes 3538952 | tf_op jit(solution)/shard_map/while/body/eval_jaxpr/ppermute | solution.py:9
  382.1 10.9 %collective-permute-start = (bf16[2,384,384]{2,1,0:T(8,128)(2,1)}, bf16[2,384,384]{2,1,0:T(8,128)(2,1)S(1)}, u32[]{:S(2)}, u32[]{:S(2)}) collective-permute-start(bf16[2,384,384]{2,1,0:T(8,128)(2,1)} %get-tuple-element.98), channel_id=1, source_target_pairs={{0,7},{1,0},{2,1},{3,2},{4,3},{5,4},{6,5},{7,6},{8,15},{9,8},{10,9... | collective-permute-start | bytes 1769480 | tf_op jit(solution)/shard_map/while/body/eval_jaxpr/ppermute | solution.py:9
  412.4 29.9 %collective-permute-start.1 = (bf16[2,2,384,384]{3,2,1,0:T(8,128)(2,1)S(1)}, bf16[2,2,384,384]{3,2,1,0:T(8,128)(2,1)}, u32[]{:S(2)}, u32[]{:S(2)}) collective-permute-start(bf16[2,2,384,384]{3,2,1,0:T(8,128)(2,1)S(1)} %copy.40), channel_id=1, source_target_pairs={{0,120},{8,0},{16,8},{24,16},{32,24},{40,32},{48,40},{56,48},{64,5... | collective-permute-start | bytes 3538952 | tf_op jit(solution)/shard_map/while/body/eval_jaxpr/ppermute | solution.py:9
  413.3 10.9 %collective-permute-start = (bf16[2,384,384]{2,1,0:T(8,128)(2,1)}, bf16[2,384,384]{2,1,0:T(8,128)(2,1)S(1)}, u32[]{:S(2)}, u32[]{:S(2)}) collective-permute-start(bf16[2,384,384]{2,1,0:T(8,128)(2,1)} %get-tuple-element.98), channel_id=1, source_target_pairs={{0,7},{1,0},{2,1},{3,2},{4,3},{5,4},{6,5},{7,6},{8,15},{9,8},{10,9... | collective-permute-start | bytes 1769480 | tf_op jit(solution)/shard_map/while/body/eval_jaxpr/ppermute | solution.py:9
  443.5 29.9 %collective-permute-start.1 = (bf16[2,2,384,384]{3,2,1,0:T(8,128)(2,1)S(1)}, bf16[2,2,384,384]{3,2,1,0:T(8,128)(2,1)}, u32[]{:S(2)}, u32[]{:S(2)}) collective-permute-start(bf16[2,2,384,384]{3,2,1,0:T(8,128)(2,1)S(1)} %copy.40), channel_id=1, source_target_pairs={{0,120},{8,0},{16,8},{24,16},{32,24},{40,32},{48,40},{56,48},{64,5... | collective-permute-start | bytes 3538952 | tf_op jit(solution)/shard_map/while/body/eval_jaxpr/ppermute | solution.py:9
  444.4 10.9 %collective-permute-start = (bf16[2,384,384]{2,1,0:T(8,128)(2,1)}, bf16[2,384,384]{2,1,0:T(8,128)(2,1)S(1)}, u32[]{:S(2)}, u32[]{:S(2)}) collective-permute-start(bf16[2,384,384]{2,1,0:T(8,128)(2,1)} %get-tuple-element.98), channel_id=1, source_target_pairs={{0,7},{1,0},{2,1},{3,2},{4,3},{5,4},{6,5},{7,6},{8,15},{9,8},{10,9... | collective-permute-start | bytes 1769480 | tf_op jit(solution)/shard_map/while/body/eval_jaxpr/ppermute | solution.py:9
  474.7 29.9 %collective-permute-start.1 = (bf16[2,2,384,384]{3,2,1,0:T(8,128)(2,1)S(1)}, bf16[2,2,384,384]{3,2,1,0:T(8,128)(2,1)}, u32[]{:S(2)}, u32[]{:S(2)}) collective-permute-start(bf16[2,2,384,384]{3,2,1,0:T(8,128)(2,1)S(1)} %copy.40), channel_id=1, source_target_pairs={{0,120},{8,0},{16,8},{24,16},{32,24},{40,32},{48,40},{56,48},{64,5... | collective-permute-start | bytes 3538952 | tf_op jit(solution)/shard_map/while/body/eval_jaxpr/ppermute | solution.py:9
  475.6 10.9 %collective-permute-start = (bf16[2,384,384]{2,1,0:T(8,128)(2,1)}, bf16[2,384,384]{2,1,0:T(8,128)(2,1)S(1)}, u32[]{:S(2)}, u32[]{:S(2)}) collective-permute-start(bf16[2,384,384]{2,1,0:T(8,128)(2,1)} %get-tuple-element.98), channel_id=1, source_target_pairs={{0,7},{1,0},{2,1},{3,2},{4,3},{5,4},{6,5},{7,6},{8,15},{9,8},{10,9... | collective-permute-start | bytes 1769480 | tf_op jit(solution)/shard_map/while/body/eval_jaxpr/ppermute | solution.py:9
  505.8 29.9 %collective-permute-start.1 = (bf16[2,2,384,384]{3,2,1,0:T(8,128)(2,1)S(1)}, bf16[2,2,384,384]{3,2,1,0:T(8,128)(2,1)}, u32[]{:S(2)}, u32[]{:S(2)}) collective-permute-start(bf16[2,2,384,384]{3,2,1,0:T(8,128)(2,1)S(1)} %copy.40), channel_id=1, source_target_pairs={{0,120},{8,0},{16,8},{24,16},{32,24},{40,32},{48,40},{56,48},{64,5... | collective-permute-start | bytes 3538952 | tf_op jit(solution)/shard_map/while/body/eval_jaxpr/ppermute | solution.py:9
  506.7 10.9 %collective-permute-start = (bf16[2,384,384]{2,1,0:T(8,128)(2,1)}, bf16[2,384,384]{2,1,0:T(8,128)(2,1)S(1)}, u32[]{:S(2)}, u32[]{:S(2)}) collective-permute-start(bf16[2,384,384]{2,1,0:T(8,128)(2,1)} %get-tuple-element.98), channel_id=1, source_target_pairs={{0,7},{1,0},{2,1},{3,2},{4,3},{5,4},{6,5},{7,6},{8,15},{9,8},{10,9... | collective-permute-start | bytes 1769480 | tf_op jit(solution)/shard_map/while/body/eval_jaxpr/ppermute | solution.py:9
  537.0 29.9 %collective-permute-start.1 = (bf16[2,2,384,384]{3,2,1,0:T(8,128)(2,1)S(1)}, bf16[2,2,384,384]{3,2,1,0:T(8,128)(2,1)}, u32[]{:S(2)}, u32[]{:S(2)}) collective-permute-start(bf16[2,2,384,384]{3,2,1,0:T(8,128)(2,1)S(1)} %copy.40), channel_id=1, source_target_pairs={{0,120},{8,0},{16,8},{24,16},{32,24},{40,32},{48,40},{56,48},{64,5... | collective-permute-start | bytes 3538952 | tf_op jit(solution)/shard_map/while/body/eval_jaxpr/ppermute | solution.py:9
  537.9 10.9 %collective-permute-start = (bf16[2,384,384]{2,1,0:T(8,128)(2,1)}, bf16[2,384,384]{2,1,0:T(8,128)(2,1)S(1)}, u32[]{:S(2)}, u32[]{:S(2)}) collective-permute-start(bf16[2,384,384]{2,1,0:T(8,128)(2,1)} %get-tuple-element.98), channel_id=1, source_target_pairs={{0,7},{1,0},{2,1},{3,2},{4,3},{5,4},{6,5},{7,6},{8,15},{9,8},{10,9... | collective-permute-start | bytes 1769480 | tf_op jit(solution)/shard_map/while/body/eval_jaxpr/ppermute | solution.py:9
  568.1 29.9 %collective-permute-start.1 = (bf16[2,2,384,384]{3,2,1,0:T(8,128)(2,1)S(1)}, bf16[2,2,384,384]{3,2,1,0:T(8,128)(2,1)}, u32[]{:S(2)}, u32[]{:S(2)}) collective-permute-start(bf16[2,2,384,384]{3,2,1,0:T(8,128)(2,1)S(1)} %copy.40), channel_id=1, source_target_pairs={{0,120},{8,0},{16,8},{24,16},{32,24},{40,32},{48,40},{56,48},{64,5... | collective-permute-start | bytes 3538952 | tf_op jit(solution)/shard_map/while/body/eval_jaxpr/ppermute | solution.py:9
  569.0 10.9 %collective-permute-start = (bf16[2,384,384]{2,1,0:T(8,128)(2,1)}, bf16[2,384,384]{2,1,0:T(8,128)(2,1)S(1)}, u32[]{:S(2)}, u32[]{:S(2)}) collective-permute-start(bf16[2,384,384]{2,1,0:T(8,128)(2,1)} %get-tuple-element.98), channel_id=1, source_target_pairs={{0,7},{1,0},{2,1},{3,2},{4,3},{5,4},{6,5},{7,6},{8,15},{9,8},{10,9... | collective-permute-start | bytes 1769480 | tf_op jit(solution)/shard_map/while/body/eval_jaxpr/ppermute | solution.py:9
  599.3 29.8 %collective-permute-start.1 = (bf16[2,2,384,384]{3,2,1,0:T(8,128)(2,1)S(1)}, bf16[2,2,384,384]{3,2,1,0:T(8,128)(2,1)}, u32[]{:S(2)}, u32[]{:S(2)}) collective-permute-start(bf16[2,2,384,384]{3,2,1,0:T(8,128)(2,1)S(1)} %copy.40), channel_id=1, source_target_pairs={{0,120},{8,0},{16,8},{24,16},{32,24},{40,32},{48,40},{56,48},{64,5... | collective-permute-start | bytes 3538952 | tf_op jit(solution)/shard_map/while/body/eval_jaxpr/ppermute | solution.py:9
  600.2 10.9 %collective-permute-start = (bf16[2,384,384]{2,1,0:T(8,128)(2,1)}, bf16[2,384,384]{2,1,0:T(8,128)(2,1)S(1)}, u32[]{:S(2)}, u32[]{:S(2)}) collective-permute-start(bf16[2,384,384]{2,1,0:T(8,128)(2,1)} %get-tuple-element.98), channel_id=1, source_target_pairs={{0,7},{1,0},{2,1},{3,2},{4,3},{5,4},{6,5},{7,6},{8,15},{9,8},{10,9... | collective-permute-start | bytes 1769480 | tf_op jit(solution)/shard_map/while/body/eval_jaxpr/ppermute | solution.py:9
  633.5 1.3 copy-start
where the time goes:
time: 637 us; the launch traced here: 636 us
  waiting for transfers between devices  490 us (77%)
  matrix products  60.1 us (9%)
  local copies, waits for them, and re-layouts  44.8 us (7%)
  starting transfers between devices  24.8 us (4%)
  other arithmetic  15.8 us (2%)
    ppermute x38, waiting for transfers between devices, passed_along(): lax.ppermute(value, axis, [(i, (i + by) % peers) for i in range(peers)])  490 us
    dot_general x16, matrix products, multiply(): jnp.einsum('otik,otkj->otij', left_side, right_side, preferred_element_ty...  60.1 us
    ppermute x38, starting transfers between devices, passed_along(): lax.ppermute(value, axis, [(i, (i + by) % peers) for i in range(peers)])  24.8 us
    while x15, local copies, waits for them, and re-layouts  19.1 us
    slice x15, local copies, waits for them, and re-layouts, west_one(): return jnp.stack([stacked[:, 1], arrived], axis=1)  14.1 us
  transfers between devices with their start and end apart: 38, of which 36 were waited for; matrix products, arithmetic and copies ran while one was open for 13% of the time, Pallas kernels for 0%

commit v1 on v0

v1 whole, which is shorter than its diff:
```python
import functools

import jax
import jax.numpy as jnp
from jax import lax
from jax.experimental import pallas as pl
from jax.experimental.pallas import tpu as pltpu
from jax.sharding import PartitionSpec as P

MESH = pl.DeviceIdType.MESH
ROWS = 384
COLS = 768
BLOCK = 64
HALF = 192
LOW = 112
HIGH = 272
WIDE = 256


def device_of(x, y, z, core):
    return (4 * z + 2 * (y // 2) + core, 2 * x + y % 2)


def spread(pattern):
    count = pattern.shape[1]
    block_of = lax.broadcasted_iota(jnp.int32, (count, COLS), 1) // BLOCK
    index = lax.broadcasted_iota(jnp.int32, (count, COLS), 0)
    select = jnp.where(block_of == index, 1.0, 0.0).astype(jnp.float32)
    return jnp.dot(pattern.astype(jnp.float32), select, preferred_element_type=jnp.float32)


def kernel(ham, den, h_pat, p_pat, keep, out, row, col, acc, send, recv):
    row_index = lax.axis_index("row")
    col_index = lax.axis_index("col")
    x, y_lo = col_index // 2, col_index % 2
    z, y_hi, core = row_index // 4, (row_index // 2) % 2, row_index % 2
    y = 2 * y_hi + y_lo
    right = device_of((x + 1) % 4, y, z, core)
    left = device_of((x + 3) % 4, y, z, core)
    up = device_of(x, y, (z + 1) % 4, core)
    down = device_of(x, y, (z + 3) % 4, core)
    beside = device_of(x, 2 * y_hi + 1 - y_lo, z, core)
    across = device_of(x, 2 * (1 - y_hi) + y_lo, z, core)
    sibling = device_of(x, y, z, 1 - core)

    barrier = pltpu.get_barrier_semaphore()
    partners = (right, left, up, down, beside, across, sibling)
    for partner in partners:
        pl.semaphore_signal(barrier, inc=1, device_id=partner, device_id_type=MESH)

    row_own = 2 * x + y_lo
    col_own = 2 * z + y_hi
    base = core * ROWS
    for matrix, (tile, pattern) in enumerate(((ham, h_pat), (den, p_pat))):
        mask = spread(pattern[...]).astype(jnp.bfloat16)
        for i in range(ROWS // BLOCK):
            rows = pl.ds(i * BLOCK, BLOCK)
            masked = tile[rows, :] * mask[i : i + 1, :]
            row[row_own, matrix, rows, :] = masked
            col[col_own, matrix, pl.ds(pl.multiple_of(base + i * BLOCK, BLOCK), BLOCK), :] = masked
    acc[...] = jnp.zeros_like(acc)
    pl.semaphore_wait(barrier, len(partners))

    started = []

    def copy(ref, target):
        index = len(started)
        made = pltpu.make_async_remote_copy(
            src_ref=ref,
            dst_ref=ref,
            send_sem=send.at[index],
            recv_sem=recv.at[index],
            device_id=target,
            device_id_type=MESH,
        )
        started.append(made)
        made.start()
        return made

    def row_part(k, first, last):
        return row.at[k, :, pl.ds(first, last - first), :]

    def col_part(k, first, last):
        start = pl.multiple_of(base + first, 16)
        return col.at[k, :, pl.ds(start, last - first), :]

    class Gather:
        def __init__(self, part, place, low, ahead, behind, partner):
            self.part, self.low = part, low
            self.place = place
            self.ahead, self.behind, self.partner = ahead, behind, partner

        def k(self, offset, other):
            low = 1 - self.low if other else self.low
            return 2 * ((self.place + offset) % 4) + low

        def send_both(self, other):
            k, part = self.k(0, other), self.part
            first = copy(part(k, 0, HALF), self.ahead)
            second = copy(part(k, HALF, ROWS), self.behind)
            third = copy(part(k, HALF, ROWS), self.ahead)
            fourth = copy(part(k, 0, HALF), self.behind)
            return first, second, third, fourth

        def send_partner(self):
            self.crossed = copy(self.part(self.k(0, False), 0, ROWS), self.partner)

        def forward(self, other, low, high):
            ahead = copy(self.part(self.k(3, other), 0, low), self.ahead)
            behind = copy(self.part(self.k(1, other), high, ROWS), self.behind)
            return ahead, behind

        def send_partner_far(self):
            self.crossed_far = copy(self.part(self.k(2, False), LOW, HIGH), self.partner)

    rows = Gather(row_part, x, y_lo, right, left, beside)
    cols = Gather(col_part, z, y_hi, up, down, across)

    def share(k):
        return copy(col_part(k, 0, ROWS), sibling)

    shared = []
    near = [g.send_both(False) for g in (rows, cols)]
    for g in (rows, cols):
        g.send_partner()
    shared.append(share(col_own))

    far = []
    for g, (first, second, third, fourth) in zip((rows, cols), near):
        first.wait_recv()
        second.wait_recv()
        far.append(g.forward(False, HALF, HALF))
    near_other = []
    for g in (rows, cols):
        g.crossed.wait_recv()
        near_other.append(g.send_both(True))
    shared.append(share(cols.k(0, True)))
    for g, (first, second, third, fourth) in zip((rows, cols), near):
        third.wait_recv()
        fourth.wait_recv()
    shared.append(share(cols.k(1, False)))
    shared.append(share(cols.k(3, False)))

    def phase_of(place, low, k):
        distance = (k // 2 - place + 4) % 4
        other = (k % 2 + low) % 2
        near_phase = jnp.where(distance == 0, 0, 2 * other)
        far_phase = 1 + 2 * other
        return jnp.where(distance == 2, far_phase, near_phase)

    def multiply(phase):
        @pl.loop(0, 8)
        def _(k):
            ready = jnp.maximum(phase_of(x, y_lo, k), phase_of(z, y_hi, k))

            @pl.when(ready == phase)
            def _():
                @pl.loop(0, COLS // WIDE)
                def _(j):
                    columns = pl.ds(pl.multiple_of(j * WIDE, WIDE), WIDE)
                    forward = jnp.dot(
                        row[k, 0], col[k, 1, :, columns], preferred_element_type=jnp.float32
                    )
                    backward = jnp.dot(
                        row[k, 1], col[k, 0, :, columns], preferred_element_type=jnp.float32
                    )
                    acc[:, columns] += forward - backward

    for made in shared:
        made.wait_recv()
    multiply(0)

    for g, (ahead, behind) in zip((rows, cols), far):
        ahead.wait_recv()
        behind.wait_recv()
        g.send_partner_far()
    last = share(cols.k(2, False))
    far_other = []
    for g, (first, second, third, fourth) in zip((rows, cols), near_other):
        first.wait_recv()
        second.wait_recv()
        far_other.append(g.forward(True, LOW, HIGH))
    last.wait_recv()
    multiply(1)

    for g, (first, second, third, fourth) in zip((rows, cols), near_other):
        third.wait_recv()
        fourth.wait_recv()
    shared = [share(cols.k(1, True)), share(cols.k(3, True))]
    for made in shared:
        made.wait_recv()
    multiply(2)

    for g, (ahead, behind) in zip((cols, rows), far_other[::-1]):
        ahead.wait_recv()
        behind.wait_recv()
        g.crossed_far.wait_recv()
        if g is cols:
            last = share(cols.k(2, True))
    last.wait_recv()
    multiply(3)

    mask = spread(keep[...])
    for i in range(ROWS // BLOCK):
        block_rows = pl.ds(i * BLOCK, BLOCK)
        out[block_rows, :] = acc[block_rows, :] * mask[i : i + 1, :]
    for made in started:
        made.wait_send()


COPIES = 36


def shards(hamiltonian, density, h_pattern, p_pattern, keep_mask):
    vmem = pl.BlockSpec(memory_space=pltpu.VMEM)
    return pl.pallas_call(
        kernel,
        out_shape=jax.ShapeDtypeStruct((ROWS, COLS), jnp.float32),
        in_specs=[vmem] * 5,
        out_specs=vmem,
        scratch_shapes=[
            pltpu.VMEM((8, 2, ROWS, COLS), jnp.bfloat16),
            pltpu.VMEM((8, 2, 2 * ROWS, COLS), jnp.bfloat16),
            pltpu.VMEM((ROWS, COLS), jnp.float32),
            pltpu.SemaphoreType.DMA((COPIES,)),
            pltpu.SemaphoreType.DMA((COPIES,)),
        ],
        compiler_params=pltpu.CompilerParams(
            collective_id=0, has_side_effects=True, vmem_limit_bytes=50 * 1024 * 1024
        ),
        name="commutator",
    )(hamiltonian, density, h_pattern, p_pattern, keep_mask)


def solution(mesh):
    return jax.shard_map(
        shards,
        mesh=mesh,
        in_specs=(
            P("row", "col"),
            P("row", "col"),
            P("row", "col"),
            P("row", "col"),
            P("row", "col"),
        ),
        out_specs=P("row", "col"),
        check_vma=False,
    )
```

time: 637 us -> 109 us (0.17)
  the two profiles are of different devices: /device:TPU:1 before, /device:TPU:8 now
where the time goes in v1:
time: 109 us
  Pallas kernels  104 us (95%)
  local copies, waits for them, and re-layouts  5.2 us (5%)
    pallas_call x1, Pallas kernels, shards(): pl.pallas_call(kernel, out_shape=jax.ShapeDtypeStruct((ROWS, COLS), jnp.f...  104 us
    unnamed x11, local copies, waits for them, and re-layouts  5.2 us

profile of v1, /device:TPU:8, one launch (start us, length us, event | category | flops | bytes accessed | tf_op | source)
XLA Modules:
  0.0 108.8 jit_solution(5848960139143469939)
XLA Ops:
  0.0 0.0 copy-start
  0.0 1.1 copy-done
  1.1 0.0 copy-start.1
  1.1 1.1 copy-done.1
  2.1 0.0 copy-start.2
  2.1 0.7 copy-done.2
  2.8 0.0 copy-start.3
  2.8 0.7 copy-done.3
  3.5 0.0 copy-start.4
  3.5 0.7 copy-done.4
  4.2 103.6 %commutator.1 = f32[384,768]{1,0:T(8,128)S(1)} custom-call(bf16[384,768]{1,0:T(8,128)(2,1)S(1)} %copy-done, bf16[384,768]{1,0:T(8,128)(2,1)S(1)} %copy-done.1, s32[6,12]{1,0:T(8,128)S(1)} %copy-done.2, s32[6,12]{1,0:T(8,128)S(1)} %copy-done.3, s32[6,12]{1,0:T(8,128)S(1)} %copy-done.4), custom_call_target="tpu_custom_call" | custom-call | tf_op jit(solution)/shard_map/commutator/pallas_call | solution.py:216
  107.8 1.0 copy.7
Async XLA Ops:
  0.0 1.1 copy-start
  1.1 1.1 copy-start.1
  2.1 0.7 copy-start.2
  2.8 0.7 copy-start.3
  3.5 0.7 copy-start.4

commit v2 on v1

v2 whole, which is shorter than its diff:
```python
import jax
import jax.numpy as jnp
from jax import lax
from jax.experimental import pallas as pl
from jax.experimental.pallas import tpu as pltpu
from jax.sharding import PartitionSpec as P

MESH = pl.DeviceIdType.MESH
ROWS = 384
COLS = 768
BLOCK = 64
BLOCK_ROWS = ROWS // BLOCK
BLOCK_COLS = COLS // BLOCK
WIDE = 256
CUTS = (0, 112, 192, 272, 384)
CHUNKS = tuple(zip(CUTS[:-1], CUTS[1:]))
WHOLE = (0, ROWS)
MIDDLE = (112, 272)
COPIES = 96


def device_of(x, y, z, core):
    return (4 * z + 2 * (y // 2) + core, 2 * x + y % 2)


def spread(pattern):
    block_of = lax.broadcasted_iota(jnp.int32, (BLOCK_COLS, COLS), 1) // BLOCK
    index = lax.broadcasted_iota(jnp.int32, (BLOCK_COLS, COLS), 0)
    select = jnp.where(block_of == index, 1.0, 0.0).astype(jnp.float32)
    return jnp.dot(pattern.astype(jnp.float32), select, preferred_element_type=jnp.float32)


class Gather:
    def __init__(self, copy, part, place, low, ahead, behind, partner):
        self.copy, self.part, self.place, self.low = copy, part, place, low
        self.ahead, self.behind, self.partner = ahead, behind, partner
        self.from_behind, self.from_ahead = {}, {}
        self.far_from_behind, self.far_from_ahead = {}, {}
        self.crossed, self.crossed_far = {}, None

    def k(self, offset, other):
        low = 1 - self.low if other else self.low
        return 2 * ((self.place + offset) % 4) + low

    def piece(self, offset, other, span):
        return self.part(self.k(offset, other), *span)

    def send_ahead(self, other, c):
        made = self.copy(self.piece(0, other, CHUNKS[c]), self.ahead)
        self.from_behind[other, c] = made

    def send_behind(self, other, c):
        made = self.copy(self.piece(0, other, CHUNKS[c]), self.behind)
        self.from_ahead[other, c] = made

    def cross(self, c):
        self.crossed[c] = self.copy(self.piece(0, False, CHUNKS[c]), self.partner)

    def pass_ahead(self, other, c):
        made = self.copy(self.piece(3, other, CHUNKS[c]), self.ahead)
        self.far_from_behind[other, c] = made

    def pass_behind(self, other, c):
        made = self.copy(self.piece(1, other, CHUNKS[c]), self.behind)
        self.far_from_ahead[other, c] = made

    def cross_far(self):
        self.crossed_far = self.copy(self.piece(2, False, MIDDLE), self.partner)


def kernel(ham, den, h_pat, p_pat, keep, out, row, col, acc, tiles, pats, send, recv, load):
    row_index = lax.axis_index("row")
    col_index = lax.axis_index("col")
    x, y_lo = col_index // 2, col_index % 2
    z, y_hi, core = row_index // 4, (row_index // 2) % 2, row_index % 2
    y = 2 * y_hi + y_lo
    right = device_of((x + 1) % 4, y, z, core)
    left = device_of((x + 3) % 4, y, z, core)
    up = device_of(x, y, (z + 1) % 4, core)
    down = device_of(x, y, (z + 3) % 4, core)
    beside = device_of(x, 2 * y_hi + 1 - y_lo, z, core)
    across = device_of(x, 2 * (1 - y_hi) + y_lo, z, core)
    sibling = device_of(x, y, z, 1 - core)

    barrier = pltpu.get_barrier_semaphore()
    partners = (right, left, up, down, beside, across, sibling)
    for partner in partners:
        pl.semaphore_signal(barrier, inc=1, device_id=partner, device_id_type=MESH)

    loads = []
    pairs = (
        (h_pat, pats.at[0]),
        (ham, tiles.at[0]),
        (p_pat, pats.at[1]),
        (den, tiles.at[1]),
        (keep, pats.at[2]),
    )
    for i, (source, target) in enumerate(pairs):
        made = pltpu.make_async_copy(source, target, load.at[i])
        made.start()
        loads.append(made)

    row_own = 2 * x + y_lo
    col_own = 2 * z + y_hi
    base = core * ROWS
    for matrix in range(2):
        loads[2 * matrix].wait()
        loads[2 * matrix + 1].wait()
        mask = spread(pats[matrix]).astype(jnp.bfloat16)
        for i in range(BLOCK_ROWS):
            rows = pl.ds(i * BLOCK, BLOCK)
            masked = tiles[matrix, rows, :] * mask[i : i + 1, :]
            row[row_own, matrix, rows, :] = masked
            col[col_own, matrix, pl.ds(pl.multiple_of(base + i * BLOCK, BLOCK), BLOCK), :] = masked
    loads[4].wait()
    pl.semaphore_wait(barrier, len(partners))

    started = []

    def copy(ref, target):
        index = len(started)
        made = pltpu.make_async_remote_copy(
            src_ref=ref,
            dst_ref=ref,
            send_sem=send.at[index],
            recv_sem=recv.at[index],
            device_id=target,
            device_id_type=MESH,
        )
        started.append(made)
        made.start()
        return made

    def row_part(k, first, last):
        return row.at[k, :, pl.ds(first, last - first), :]

    def col_part(k, first, last):
        start = pl.multiple_of(base + first, 16)
        return col.at[k, :, pl.ds(start, last - first), :]

    rows = Gather(copy, row_part, x, y_lo, right, left, beside)
    cols = Gather(copy, col_part, z, y_hi, up, down, across)
    both = (rows, cols)
    shared = []

    def share(offset, other, span):
        shared.append(copy(cols.piece(offset, other, span), sibling))

    def wait_shared():
        for made in shared:
            made.wait_recv()
        shared.clear()

    def phase_of(place, low, k):
        distance = (k // 2 - place + 4) % 4
        other = (k % 2 + low) % 2
        near = jnp.where(distance == 0, 2, 3)
        own_ring = jnp.where(distance == 2, 1, 0)
        other_ring = jnp.where(distance == 2, 4, near)
        return jnp.where(other == 0, own_ring, other_ring)

    def multiply(phase):
        @pl.loop(0, 8)
        def _(k):
            ready = jnp.maximum(phase_of(x, y_lo, k), phase_of(z, y_hi, k))

            @pl.when(ready == phase)
            def _():
                @pl.loop(0, COLS // WIDE)
                def _(j):
                    columns = pl.ds(pl.multiple_of(j * WIDE, WIDE), WIDE)
                    forward = jnp.dot(
                        row[k, 0], col[k, 1, :, columns], preferred_element_type=jnp.float32
                    )
                    backward = jnp.dot(
                        row[k, 1], col[k, 0, :, columns], preferred_element_type=jnp.float32
                    )
                    acc[:, columns] += forward - backward

    for first, second in ((0, 3), (1, 2), (2, 1), (3, 0)):
        for g in both:
            g.send_ahead(False, first)
            g.send_behind(False, second)
            if first == 0:
                g.cross(0)
                g.cross(3)
    for g in both:
        g.cross(1)
        g.cross(2)
    share(0, False, WHOLE)
    acc[...] = jnp.zeros_like(acc)

    for first, second in ((0, 3), (1, 2)):
        for g in both:
            g.from_behind[False, first].wait_recv()
            g.pass_ahead(False, first)
            g.from_ahead[False, second].wait_recv()
            g.pass_behind(False, second)
    for c in (0, 3):
        for g in both:
            g.crossed[c].wait_recv()
            if c == 0:
                g.send_ahead(True, 0)
            else:
                g.send_behind(True, 3)
                g.send_ahead(True, 3)
                g.send_behind(True, 0)

    for first, second in ((2, 1), (3, 0)):
        for g in both:
            g.from_behind[False, first].wait_recv()
            g.from_ahead[False, second].wait_recv()
    share(3, False, WHOLE)
    share(1, False, WHOLE)
    wait_shared()
    multiply(0)

    for g in both:
        g.crossed[1].wait_recv()
        g.send_ahead(True, 1)
        g.send_behind(True, 1)
    for first, second in ((0, 3), (1, 2)):
        for g in both:
            g.far_from_behind[False, first].wait_recv()
            g.far_from_ahead[False, second].wait_recv()
    for g in both:
        g.cross_far()
    share(2, False, WHOLE)
    for g in both:
        g.crossed[2].wait_recv()
        g.send_ahead(True, 2)
        g.send_behind(True, 2)
    share(0, True, WHOLE)
    for g in both:
        g.from_behind[True, 0].wait_recv()
        g.pass_ahead(True, 0)
        g.from_ahead[True, 3].wait_recv()
        g.pass_behind(True, 3)
    wait_shared()
    multiply(1)
    multiply(2)

    for first, second in ((3, 0), (1, 1)):
        for g in both:
            g.from_behind[True, first].wait_recv()
            g.from_ahead[True, second].wait_recv()
    share(3, True, (0, 192))
    share(3, True, (272, 384))
    share(1, True, (0, 192))
    share(1, True, (272, 384))
    for g in both:
        g.from_behind[True, 2].wait_recv()
        g.from_ahead[True, 2].wait_recv()
    share(3, True, (192, 272))
    share(1, True, (192, 272))
    wait_shared()
    multiply(3)

    cols.crossed_far.wait_recv()
    share(2, True, MIDDLE)
    cols.far_from_behind[True, 0].wait_recv()
    share(2, True, CHUNKS[0])
    cols.far_from_ahead[True, 3].wait_recv()
    share(2, True, CHUNKS[3])
    rows.crossed_far.wait_recv()
    rows.far_from_behind[True, 0].wait_recv()
    rows.far_from_ahead[True, 3].wait_recv()
    wait_shared()
    multiply(4)

    mask = spread(pats[2])
    for i in range(BLOCK_ROWS):
        block_rows = pl.ds(i * BLOCK, BLOCK)
        out[block_rows, :] = acc[block_rows, :] * mask[i : i + 1, :]
    for made in started:
        made.wait_send()


def shards(hamiltonian, density, h_pattern, p_pattern, keep_mask):
    return pl.pallas_call(
        kernel,
        out_shape=jax.ShapeDtypeStruct((ROWS, COLS), jnp.float32),
        in_specs=[pl.BlockSpec(memory_space=pl.ANY)] * 5,
        out_specs=pl.BlockSpec(memory_space=pltpu.VMEM),
        scratch_shapes=[
            pltpu.VMEM((8, 2, ROWS, COLS), jnp.bfloat16),
            pltpu.VMEM((8, 2, 2 * ROWS, COLS), jnp.bfloat16),
            pltpu.VMEM((ROWS, COLS), jnp.float32),
            pltpu.VMEM((2, ROWS, COLS), jnp.bfloat16),
            pltpu.VMEM((3, BLOCK_ROWS, BLOCK_COLS), jnp.int32),
            pltpu.SemaphoreType.DMA((COPIES,)),
            pltpu.SemaphoreType.DMA((COPIES,)),
            pltpu.SemaphoreType.DMA((5,)),
        ],
        compiler_params=pltpu.CompilerParams(
            collective_id=0, has_side_effects=True, vmem_limit_bytes=60 * 1024 * 1024
        ),
        name="commutator",
    )(hamiltonian, density, h_pattern, p_pattern, keep_mask)


def solution(mesh):
    return jax.shard_map(
        shards,
        mesh=mesh,
        in_specs=(
            P("row", "col"),
            P("row", "col"),
            P("row", "col"),
            P("row", "col"),
            P("row", "col"),
        ),
        out_specs=P("row", "col"),
        check_vma=False,
    )
```

time: 109 us -> 90.9 us (0.83)
  the two profiles are of different devices: /device:TPU:8 before, /device:TPU:1 now
where the time goes in v2:
time: 90.9 us; the launch traced here: 90 us
  Pallas kernels  87.7 us (96%)
  local copies, waits for them, and re-layouts  2.36 us (3%)
    pallas_call x1, Pallas kernels, shards(): pl.pallas_call(kernel, out_shape=jax.ShapeDtypeStruct((ROWS, COLS), jnp.f...  87.7 us
    unnamed x1, local copies, waits for them, and re-layouts  2.36 us

profile of v2, /device:TPU:1, one launch (start us, length us, event | category | flops | bytes accessed | tf_op | source)
XLA Modules:
  0.0 90.0 jit_solution(16468991355132409957)
XLA Ops:
  0.0 87.7 %commutator.1 = f32[384,768]{1,0:T(8,128)} custom-call(bf16[384,768]{1,0:T(8,128)(2,1)} %ham.1, bf16[384,768]{1,0:T(8,128)(2,1)} %den.1, s32[6,12]{1,0:T(8,128)} %h_pat.1, s32[6,12]{1,0:T(8,128)} %p_pat.1, s32[6,12]{1,0:T(8,128)} %keep.1), custom_call_target="tpu_custom_call" | custom-call | tf_op jit(solution)/shard_map/commutator/pallas_call | solution.py:280
  87.7 2.4 %copy.7 = f32[384,768]{1,0:T(8,128)} copy(f32[384,768]{1,0:T(8,128)} %commutator.1) | data formatting | bytes 2359296

commit v3 on v2

v3 whole, which is shorter than its diff:
```python
import jax
import jax.numpy as jnp
from jax import lax
from jax.experimental import pallas as pl
from jax.experimental.pallas import tpu as pltpu
from jax.sharding import PartitionSpec as P

MESH = pl.DeviceIdType.MESH
ROWS = 384
COLS = 768
BLOCK = 64
BLOCK_ROWS = ROWS // BLOCK
BLOCK_COLS = COLS // BLOCK
CUTS = (0, 128, 192, 256, 384)
CHUNKS = tuple(zip(CUTS[:-1], CUTS[1:]))
WHOLE = (0, ROWS)
LOW = (0, 48)
MIDDLE = (48, 192)
UPPER = (192, 336)
HIGH = (336, 384)
COPIES = 96


def device_of(x, y, z, core):
    return (4 * z + 2 * (y // 2) + core, 2 * x + y % 2)


def spread(pattern):
    block_of = lax.broadcasted_iota(jnp.int32, (BLOCK_COLS, COLS), 1) // BLOCK
    index = lax.broadcasted_iota(jnp.int32, (BLOCK_COLS, COLS), 0)
    select = jnp.where(block_of == index, 1.0, 0.0).astype(jnp.float32)
    return jnp.dot(pattern.astype(jnp.float32), select, preferred_element_type=jnp.float32)


class Gather:
    def __init__(self, copy, part, place, low, ahead, behind):
        self.copy, self.part, self.place, self.low = copy, part, place, low
        self.ahead, self.behind = ahead, behind
        self.from_behind, self.from_ahead = {}, {}
        self.far_from_behind, self.far_from_ahead = {}, {}

    def k(self, offset, other):
        low = 1 - self.low if other else self.low
        return 2 * ((self.place + offset) % 4) + low

    def piece(self, offset, other, span):
        return self.part(self.k(offset, other), *span)

    def send_ahead(self, other, c):
        piece = self.piece(0, other, CHUNKS[c])
        self.from_behind[other, c] = self.copy(piece, piece, self.ahead)

    def send_behind(self, other, c):
        piece = self.piece(0, other, CHUNKS[c])
        self.from_ahead[other, c] = self.copy(piece, piece, self.behind)

    def pass_ahead(self, other, c, span):
        piece = self.piece(3, other, span)
        self.far_from_behind[other, c] = self.copy(piece, piece, self.ahead)

    def pass_behind(self, other, c, span):
        piece = self.piece(1, other, span)
        self.far_from_ahead[other, c] = self.copy(piece, piece, self.behind)


def kernel(ham, den, h_pat, p_pat, keep, out, row, col, acc, tiles, pats, send, recv, load):
    row_index = lax.axis_index("row")
    col_index = lax.axis_index("col")
    x, y_lo = col_index // 2, col_index % 2
    z, y_hi, core = row_index // 4, (row_index // 2) % 2, row_index % 2
    y = 2 * y_hi + y_lo
    right = device_of((x + 1) % 4, y, z, core)
    left = device_of((x + 3) % 4, y, z, core)
    up = device_of(x, y, (z + 1) % 4, core)
    down = device_of(x, y, (z + 3) % 4, core)
    beside = device_of(x, 2 * y_hi + 1 - y_lo, z, core)
    across = device_of(x, 2 * (1 - y_hi) + y_lo, z, core)
    opposite = device_of(x, 3 - y, z, core)
    sibling = device_of(x, y, z, 1 - core)

    barrier = pltpu.get_barrier_semaphore()
    partners = (right, left, up, down, beside, across, opposite, sibling)
    for partner in partners:
        pl.semaphore_signal(barrier, inc=1, device_id=partner, device_id_type=MESH)

    loads = []
    pairs = (
        (h_pat, pats.at[0]),
        (ham, tiles.at[0]),
        (p_pat, pats.at[1]),
        (den, tiles.at[1]),
        (keep, pats.at[2]),
    )
    for i, (source, target) in enumerate(pairs):
        made = pltpu.make_async_copy(source, target, load.at[i])
        made.start()
        loads.append(made)

    row_own = 2 * x + y_lo
    col_own = 2 * z + y_hi
    base = core * ROWS
    for matrix in range(2):
        loads[2 * matrix].wait()
        loads[2 * matrix + 1].wait()
        mask = spread(pats[matrix]).astype(jnp.bfloat16)
        for i in range(BLOCK_ROWS):
            rows = pl.ds(i * BLOCK, BLOCK)
            masked = tiles[matrix, rows, :] * mask[i : i + 1, :]
            row[row_own, matrix, rows, :] = masked
            col[col_own, matrix, pl.ds(pl.multiple_of(base + i * BLOCK, BLOCK), BLOCK), :] = masked
    loads[4].wait()
    pl.semaphore_wait(barrier, len(partners))

    started = []

    def copy(source, landing, target):
        index = len(started)
        made = pltpu.make_async_remote_copy(
            src_ref=source,
            dst_ref=landing,
            send_sem=send.at[index],
            recv_sem=recv.at[index],
            device_id=target,
            device_id_type=MESH,
        )
        started.append(made)
        made.start()
        return made

    def row_part(k, first, last):
        return row.at[k, :, pl.ds(first, last - first), :]

    def col_part(k, first, last):
        start = pl.multiple_of(base + first, 16)
        return col.at[k, :, pl.ds(start, last - first), :]

    rows = Gather(copy, row_part, x, y_lo, right, left)
    cols = Gather(copy, col_part, z, y_hi, up, down)
    both = (rows, cols)
    shared = []

    def share(offset, other, span):
        piece = cols.piece(offset, other, span)
        shared.append(copy(piece, piece, sibling))

    def wait_shared():
        for made in shared:
            made.wait_recv()
        shared.clear()

    crossed, turned = {}, {}

    def cross(c):
        piece = rows.piece(0, False, CHUNKS[c])
        crossed[c] = copy(piece, piece, beside)

    def turn(c):
        crossed[c].wait_recv()
        landing = col_part(col_own, *CHUNKS[c])
        turned[c] = copy(rows.piece(0, True, CHUNKS[c]), landing, opposite)

    def phase_of(place, low, k):
        distance = (k // 2 - place + 4) % 4
        other = (k % 2 + low) % 2
        late = jnp.where(distance == 2, 2, 1)
        return jnp.where((other == 0) | (distance == 0), 0, late)

    def multiply(phase):
        @pl.loop(0, 8)
        def _(k):
            ready = jnp.maximum(phase_of(x, y_lo, k), phase_of(z, y_hi, k))

            @pl.when(ready == phase)
            def _():
                forward = jnp.dot(row[k, 0], col[k, 1], preferred_element_type=jnp.float32)
                backward = jnp.dot(row[k, 1], col[k, 0], preferred_element_type=jnp.float32)
                acc[...] += forward - backward

    for first, second in ((0, 3), (1, 2)):
        for g in both:
            g.send_ahead(False, first)
            g.send_behind(False, second)
        cross(first)
        cross(second)
    share(0, False, WHOLE)
    acc[...] = jnp.zeros_like(acc)

    for first, second in ((0, 3), (1, 2)):
        for g in both:
            g.from_behind[False, first].wait_recv()
            g.pass_ahead(False, first, CHUNKS[first])
            g.from_ahead[False, second].wait_recv()
            g.pass_behind(False, second, CHUNKS[second])
        turn(first)
    for first, second in ((2, 1), (3, 0)):
        for g in both:
            g.send_ahead(False, first)
            g.send_behind(False, second)
    turn(3)
    turn(2)

    for c in range(4):
        rows.send_ahead(True, c)
        rows.send_behind(True, 3 - c)
    far = {}
    for first, second in ((0, 3), (1, 2)):
        for c in (first, second):
            turned[c].wait_recv()
            cols.send_ahead(True, c)
            cols.send_behind(True, c)
    share(0, True, WHOLE)
    for first, second in ((0, 3), (1, 2)):
        for g in both:
            g.far_from_behind[False, first].wait_recv()
            g.far_from_ahead[False, second].wait_recv()
    for span in (MIDDLE, UPPER):
        for g, target in ((rows, beside), (cols, across)):
            piece = g.piece(2, False, span)
            far[g, span] = copy(piece, piece, target)
    share(2, False, WHOLE)
    for first, second in ((2, 1), (3, 0)):
        for g in both:
            g.from_behind[False, first].wait_recv()
            g.from_ahead[False, second].wait_recv()
    share(3, False, WHOLE)
    share(1, False, WHOLE)
    for g in both:
        g.from_behind[True, 0].wait_recv()
        g.pass_ahead(True, 0, LOW)
        g.from_ahead[True, 3].wait_recv()
        g.pass_behind(True, 3, HIGH)
    wait_shared()
    multiply(0)

    for g in both:
        for c in (1, 2):
            g.from_behind[True, c].wait_recv()
            g.from_ahead[True, 3 - c].wait_recv()
        if g is cols:
            g.from_behind[True, 3].wait_recv()
            g.from_ahead[True, 0].wait_recv()
            share(3, True, WHOLE)
            share(1, True, WHOLE)
    rows.from_behind[True, 3].wait_recv()
    rows.from_ahead[True, 0].wait_recv()
    wait_shared()
    multiply(1)

    for span in (MIDDLE, UPPER):
        for g in both:
            far[g, span].wait_recv()
    share(2, True, (MIDDLE[0], UPPER[1]))
    cols.far_from_behind[True, 0].wait_recv()
    share(2, True, LOW)
    cols.far_from_ahead[True, 3].wait_recv()
    share(2, True, HIGH)
    rows.far_from_behind[True, 0].wait_recv()
    rows.far_from_ahead[True, 3].wait_recv()
    wait_shared()
    multiply(2)

    mask = spread(pats[2])
    for i in range(BLOCK_ROWS):
        block_rows = pl.ds(i * BLOCK, BLOCK)
        out[block_rows, :] = acc[block_rows, :] * mask[i : i + 1, :]
    for made in started:
        made.wait_send()


def shards(hamiltonian, density, h_pattern, p_pattern, keep_mask):
    return pl.pallas_call(
        kernel,
        out_shape=jax.ShapeDtypeStruct((ROWS, COLS), jnp.float32),
        in_specs=[pl.BlockSpec(memory_space=pl.ANY)] * 5,
        out_specs=pl.BlockSpec(memory_space=pltpu.VMEM),
        scratch_shapes=[
            pltpu.VMEM((8, 2, ROWS, COLS), jnp.bfloat16),
            pltpu.VMEM((8, 2, 2 * ROWS, COLS), jnp.bfloat16),
            pltpu.VMEM((ROWS, COLS), jnp.float32),
            pltpu.VMEM((2, ROWS, COLS), jnp.bfloat16),
            pltpu.VMEM((3, BLOCK_ROWS, BLOCK_COLS), jnp.int32),
            pltpu.SemaphoreType.DMA((COPIES,)),
            pltpu.SemaphoreType.DMA((COPIES,)),
            pltpu.SemaphoreType.DMA((5,)),
        ],
        compiler_params=pltpu.CompilerParams(
            collective_id=0, has_side_effects=True, vmem_limit_bytes=60 * 1024 * 1024
        ),
        name="commutator",
    )(hamiltonian, density, h_pattern, p_pattern, keep_mask)


def solution(mesh):
    return jax.shard_map(
        shards,
        mesh=mesh,
        in_specs=(
            P("row", "col"),
            P("row", "col"),
            P("row", "col"),
            P("row", "col"),
            P("row", "col"),
        ),
        out_specs=P("row", "col"),
        check_vma=False,
    )
```

time: 90.9 us -> 93.2 us (1.025)
  Pallas kernels: 87.7 us -> 90.3 us
    pallas_call x1, Pallas kernels: 87.7 us -> 90.3 us  [shards(): pl.pallas_call(kernel, out_shape=jax.ShapeDtypeStruct((ROWS, COLS), jnp.f...]
where the time goes in v3:
time: 93.2 us; the launch traced here: 92.6 us
  Pallas kernels  90.3 us (97%)
  local copies, waits for them, and re-layouts  2.36 us (3%)
    pallas_call x1, Pallas kernels, shards(): pl.pallas_call(kernel, out_shape=jax.ShapeDtypeStruct((ROWS, COLS), jnp.f...  90.3 us
    unnamed x1, local copies, waits for them, and re-layouts  2.36 us

profile of v3, /device:TPU:1, one launch (start us, length us, event | category | flops | bytes accessed | tf_op | source)
XLA Modules:
  0.0 92.6 jit_solution(18257039099297534008)
XLA Ops:
  0.0 90.3 %commutator.1 = f32[384,768]{1,0:T(8,128)} custom-call(bf16[384,768]{1,0:T(8,128)(2,1)} %ham.1, bf16[384,768]{1,0:T(8,128)(2,1)} %den.1, s32[6,12]{1,0:T(8,128)} %h_pat.1, s32[6,12]{1,0:T(8,128)} %p_pat.1, s32[6,12]{1,0:T(8,128)} %keep.1), custom_call_target="tpu_custom_call" | custom-call | tf_op jit(solution)/shard_map/commutator/pallas_call | solution.py:271
  90.3 2.4 %copy.7 = f32[384,768]{1,0:T(8,128)} copy(f32[384,768]{1,0:T(8,128)} %commutator.1) | data formatting | bytes 2359296

commit v4 on v3

--- a/solution.py
+++ b/solution.py
@@ -14,10 +14,11 @@
 CUTS = (0, 128, 192, 256, 384)
 CHUNKS = tuple(zip(CUTS[:-1], CUTS[1:]))
 WHOLE = (0, ROWS)
-LOW = (0, 48)
-MIDDLE = (48, 192)
-UPPER = (192, 336)
-HIGH = (336, 384)
+LOW = (0, 64)
+MIDDLE = (64, 192)
+UPPER = (192, 320)
+HIGH = (320, 384)
+TAIL = 128
 COPIES = 96
 
 
@@ -159,22 +160,91 @@
         landing = col_part(col_own, *CHUNKS[c])
         turned[c] = copy(rows.piece(0, True, CHUNKS[c]), landing, opposite)
 
-    def phase_of(place, low, k):
+    def kind_of(place, low, k):
         distance = (k // 2 - place + 4) % 4
         other = (k % 2 + low) % 2
         late = jnp.where(distance == 2, 2, 1)
         return jnp.where((other == 0) | (distance == 0), 0, late)
 
-    def multiply(phase):
+    def offset_of(place, k):
+        behind = (k // 2 - place + 4) % 4 == 3
+        return jnp.where(behind, 0, TAIL), jnp.where(behind, ROWS - TAIL, 0)
+
+    def product(k, first, count, inner, depth):
+        out_rows = pl.ds(pl.multiple_of(first, TAIL), count)
+
+        def left(matrix):
+            if depth == ROWS:
+                return row[k, matrix, out_rows, :]
+            spans = [pl.ds(pl.multiple_of(i * ROWS + inner, TAIL), depth) for i in range(2)]
+            return jnp.concatenate([row[k, matrix, out_rows, span] for span in spans], axis=1)
+
+        def right(matrix):
+            if depth == ROWS:
+                return col[k, matrix]
+            spans = [pl.ds(pl.multiple_of(i * ROWS + inner, TAIL), depth) for i in range(2)]
+            return jnp.concatenate([col[k, matrix, span, :] for span in spans], axis=0)
+
+        forward = jnp.dot(left(0), right(1), preferred_element_type=jnp.float32)
+        backward = jnp.dot(left(1), right(0), preferred_element_type=jnp.float32)
+        acc[out_rows, :] += forward - backward
+
+    def over_blocks(body):
         @pl.loop(0, 8)
         def _(k):
-            ready = jnp.maximum(phase_of(x, y_lo, k), phase_of(z, y_hi, k))
-
-            @pl.when(ready == phase)
+            body(k, kind_of(x, y_lo, k), kind_of(z, y_hi, k))
+
+    def multiply_early(k, r, c):
+        @pl.when((r == 0) & (c == 0))
+        def _():
+            product(k, 0, ROWS, 0, ROWS)
+
+    def multiply_first(row_other, col_other):
+        def body(k, r, c):
+            row_start, _ = offset_of(x, k)
+            col_start, _ = offset_of(z, k)
+
+            @pl.when((r == 1) & (c == col_other))
             def _():
-                forward = jnp.dot(row[k, 0], col[k, 1], preferred_element_type=jnp.float32)
-                backward = jnp.dot(row[k, 1], col[k, 0], preferred_element_type=jnp.float32)
-                acc[...] += forward - backward
+                product(k, row_start, ROWS - TAIL, 0, ROWS)
+
+            @pl.when((r == row_other) & (c == 1))
+            def _():
+                product(k, 0, ROWS, col_start, ROWS - TAIL)
+
+            if row_other == 0:
+
+                @pl.when((r == 1) & (c == 1))
+                def _():
+                    product(k, row_start, ROWS - TAIL, col_start, ROWS - TAIL)
+
+            else:
+
+                @pl.when(((r == 2) & (c != 1)) | ((r != 1) & (c == 2)))
+                def _():
+                    product(k, 0, ROWS, 0, ROWS)
+
+        return body
+
+    def multiply_last_rows(k, r, c):
+        _, row_start = offset_of(x, k)
+
+        @pl.when((r == 1) & (c != 1))
+        def _():
+            product(k, row_start, TAIL, 0, ROWS)
+
+    def multiply_last(k, r, c):
+        row_first, row_start = offset_of(x, k)
+        _, col_start = offset_of(z, k)
+
+        @pl.when((r == 1) & (c == 1))
+        def _():
+            product(k, row_start, TAIL, 0, ROWS)
+            product(k, row_first, ROWS - TAIL, col_start, TAIL)
+
+        @pl.when((r != 1) & (c == 1))
+        def _():
+            product(k, 0, ROWS, col_start, TAIL)
 
     for first, second in ((0, 3), (1, 2)):
         for g in both:
@@ -191,24 +261,19 @@
             g.pass_ahead(False, first, CHUNKS[first])
             g.from_ahead[False, second].wait_recv()
             g.pass_behind(False, second, CHUNKS[second])
-        turn(first)
+        if first == 0:
+            turn(0)
     for first, second in ((2, 1), (3, 0)):
         for g in both:
             g.send_ahead(False, first)
             g.send_behind(False, second)
-    turn(3)
-    turn(2)
-
-    for c in range(4):
+    for c in (3, 1, 2):
+        turn(c)
+
+    for c in range(3):
         rows.send_ahead(True, c)
         rows.send_behind(True, 3 - c)
     far = {}
-    for first, second in ((0, 3), (1, 2)):
-        for c in (first, second):
-            turned[c].wait_recv()
-            cols.send_ahead(True, c)
-            cols.send_behind(True, c)
-    share(0, True, WHOLE)
     for first, second in ((0, 3), (1, 2)):
         for g in both:
             g.far_from_behind[False, first].wait_recv()
@@ -218,6 +283,17 @@
             piece = g.piece(2, False, span)
             far[g, span] = copy(piece, piece, target)
     share(2, False, WHOLE)
+    turned[0].wait_recv()
+    cols.send_ahead(True, 0)
+    turned[3].wait_recv()
+    cols.send_behind(True, 3)
+    turned[1].wait_recv()
+    cols.send_ahead(True, 1)
+    turned[2].wait_recv()
+    cols.send_ahead(True, 2)
+    cols.send_behind(True, 2)
+    cols.send_behind(True, 1)
+    share(0, True, WHOLE)
     for first, second in ((2, 1), (3, 0)):
         for g in both:
             g.from_behind[False, first].wait_recv()
@@ -227,37 +303,46 @@
     for g in both:
         g.from_behind[True, 0].wait_recv()
         g.pass_ahead(True, 0, LOW)
+        g.send_ahead(True, 3)
         g.from_ahead[True, 3].wait_recv()
         g.pass_behind(True, 3, HIGH)
+        g.send_behind(True, 0)
     wait_shared()
-    multiply(0)
-
-    for g in both:
+    over_blocks(multiply_early)
+
+    for g in (cols, rows):
         for c in (1, 2):
             g.from_behind[True, c].wait_recv()
             g.from_ahead[True, 3 - c].wait_recv()
         if g is cols:
-            g.from_behind[True, 3].wait_recv()
-            g.from_ahead[True, 0].wait_recv()
-            share(3, True, WHOLE)
-            share(1, True, WHOLE)
-    rows.from_behind[True, 3].wait_recv()
-    rows.from_ahead[True, 0].wait_recv()
+            share(3, True, (0, ROWS - TAIL))
+            share(1, True, (TAIL, ROWS))
     wait_shared()
-    multiply(1)
+    over_blocks(multiply_first(0, 0))
 
     for span in (MIDDLE, UPPER):
-        for g in both:
-            far[g, span].wait_recv()
-    share(2, True, (MIDDLE[0], UPPER[1]))
+        far[cols, span].wait_recv()
+        share(2, True, span)
     cols.far_from_behind[True, 0].wait_recv()
     share(2, True, LOW)
     cols.far_from_ahead[True, 3].wait_recv()
     share(2, True, HIGH)
+    for span in (MIDDLE, UPPER):
+        far[rows, span].wait_recv()
     rows.far_from_behind[True, 0].wait_recv()
     rows.far_from_ahead[True, 3].wait_recv()
     wait_shared()
-    multiply(2)
+    over_blocks(multiply_first(2, 2))
+
+    cols.from_behind[True, 3].wait_recv()
+    share(3, True, CHUNKS[3])
+    cols.from_ahead[True, 0].wait_recv()
+    share(1, True, CHUNKS[0])
+    rows.from_behind[True, 3].wait_recv()
+    rows.from_ahead[True, 0].wait_recv()
+    over_blocks(multiply_last_rows)
+    wait_shared()
+    over_blocks(multiply_last)
 
     mask = spread(pats[2])
     for i in range(BLOCK_ROWS):

time: 93.2 us -> 85.5 us (0.917)
  Pallas kernels: 90.3 us -> 82.9 us
    pallas_call x1, Pallas kernels: 90.3 us -> 82.9 us  [shards(): pl.pallas_call(kernel, out_shape=jax.ShapeDtypeStruct((ROWS, COLS), jnp.f...]
where the time goes in v4:
time: 85.5 us; the launch traced here: 85.3 us
  Pallas kernels  82.9 us (97%)
  local copies, waits for them, and re-layouts  2.36 us (3%)
    pallas_call x1, Pallas kernels, shards(): pl.pallas_call(kernel, out_shape=jax.ShapeDtypeStruct((ROWS, COLS), jnp.f...  82.9 us
    unnamed x1, local copies, waits for them, and re-layouts  2.36 us

profile of v4, /device:TPU:1, one launch (start us, length us, event | category | flops | bytes accessed | tf_op | source)
XLA Modules:
  0.0 85.3 jit_solution(16573141743365530625)
XLA Ops:
  0.0 82.9 %commutator.1 = f32[384,768]{1,0:T(8,128)} custom-call(bf16[384,768]{1,0:T(8,128)(2,1)} %ham.1, bf16[384,768]{1,0:T(8,128)(2,1)} %den.1, s32[6,12]{1,0:T(8,128)} %h_pat.1, s32[6,12]{1,0:T(8,128)} %p_pat.1, s32[6,12]{1,0:T(8,128)} %keep.1), custom_call_target="tpu_custom_call" | custom-call | tf_op jit(solution)/shard_map/commutator/pallas_call | solution.py:356
  82.9 2.4 %copy.7 = f32[384,768]{1,0:T(8,128)} copy(f32[384,768]{1,0:T(8,128)} %commutator.1) | data formatting | bytes 2359296

commit v5 on v4

--- a/solution.py
+++ b/solution.py
@@ -15,11 +15,10 @@
 CHUNKS = tuple(zip(CUTS[:-1], CUTS[1:]))
 WHOLE = (0, ROWS)
 LOW = (0, 64)
-MIDDLE = (64, 192)
-UPPER = (192, 320)
+MIDDLE = ((64, 128), (128, 192), (192, 256), (256, 320))
 HIGH = (320, 384)
 TAIL = 128
-COPIES = 96
+ARRIVALS = 38
 
 
 def device_of(x, y, z, core):
@@ -34,11 +33,18 @@
 
 
 class Gather:
-    def __init__(self, copy, part, place, low, ahead, behind):
+    def __init__(self, copy, arrival, part, place, low, ahead, behind):
         self.copy, self.part, self.place, self.low = copy, part, place, low
         self.ahead, self.behind = ahead, behind
-        self.from_behind, self.from_ahead = {}, {}
-        self.far_from_behind, self.far_from_ahead = {}, {}
+        first, second, third, fourth, last = (arrival() for _ in range(5))
+        self.from_behind = {(False, 0): first, (False, 1): second, (False, 2): last, (False, 3): last}
+        self.from_ahead = {(False, 3): third, (False, 2): fourth, (False, 1): last, (False, 0): last}
+        first, second, middle, last = (arrival() for _ in range(4))
+        self.from_behind.update({(True, 0): first, (True, 1): middle, (True, 2): middle, (True, 3): last})
+        self.from_ahead.update({(True, 3): second, (True, 2): middle, (True, 1): middle, (True, 0): last})
+        outer, inner = arrival(), arrival()
+        self.far = {0: outer, 3: outer, 1: inner, 2: inner}
+        self.far_passed, self.far_crossed = arrival(), arrival()
 
     def k(self, offset, other):
         low = 1 - self.low if other else self.low
@@ -47,21 +53,32 @@
     def piece(self, offset, other, span):
         return self.part(self.k(offset, other), *span)
 
+    def move(self, offset, other, span, target, arrival):
+        piece = self.piece(offset, other, span)
+        self.copy(piece, piece, target, span, arrival)
+
     def send_ahead(self, other, c):
-        piece = self.piece(0, other, CHUNKS[c])
-        self.from_behind[other, c] = self.copy(piece, piece, self.ahead)
+        self.move(0, other, CHUNKS[c], self.ahead, self.from_behind[other, c])
 
     def send_behind(self, other, c):
-        piece = self.piece(0, other, CHUNKS[c])
-        self.from_ahead[other, c] = self.copy(piece, piece, self.behind)
-
-    def pass_ahead(self, other, c, span):
-        piece = self.piece(3, other, span)
-        self.far_from_behind[other, c] = self.copy(piece, piece, self.ahead)
-
-    def pass_behind(self, other, c, span):
-        piece = self.piece(1, other, span)
-        self.far_from_ahead[other, c] = self.copy(piece, piece, self.behind)
+        self.move(0, other, CHUNKS[c], self.behind, self.from_ahead[other, c])
+
+    def pass_ahead(self, c):
+        self.move(3, False, CHUNKS[c], self.ahead, self.far[c])
+
+    def pass_behind(self, c):
+        self.move(1, False, CHUNKS[c], self.behind, self.far[c])
+
+    def pass_edges(self):
+        self.from_behind[True, 0].wait()
+        self.move(3, True, LOW, self.ahead, self.far_passed)
+        self.send_ahead(True, 3)
+        self.from_ahead[True, 3].wait()
+        self.move(1, True, HIGH, self.behind, self.far_passed)
+        self.send_behind(True, 0)
+
+    def cross_far(self, c, target):
+        self.move(2, False, MIDDLE[c], target, self.far_crossed)
 
 
 def kernel(ham, den, h_pat, p_pat, keep, out, row, col, acc, tiles, pats, send, recv, load):
@@ -112,21 +129,47 @@
     loads[4].wait()
     pl.semaphore_wait(barrier, len(partners))
 
-    started = []
-
-    def copy(source, landing, target):
-        index = len(started)
-        made = pltpu.make_async_remote_copy(
+    def extent(count):
+        if count <= 2 * ROWS:
+            return col.at[0, :, pl.ds(0, count), :]
+        if count <= 8 * ROWS:
+            return row.at[pl.ds(0, count // ROWS)]
+        return col.at[pl.ds(0, count // (2 * ROWS))]
+
+    def described(source, landing, target, sender, arrival):
+        return pltpu.make_async_remote_copy(
             src_ref=source,
             dst_ref=landing,
-            send_sem=send.at[index],
-            recv_sem=recv.at[index],
+            send_sem=send.at[sender],
+            recv_sem=recv.at[arrival],
             device_id=target,
             device_id_type=MESH,
         )
-        started.append(made)
-        made.start()
-        return made
+
+    arrivals = []
+
+    class Arrival:
+        def __init__(self):
+            self.index, self.count = len(arrivals), 0
+            arrivals.append(self)
+
+        def wait(self):
+            if self.count:
+                area = extent(self.count)
+                described(area, area, sibling, 0, self.index).wait_recv()
+                self.count = 0
+
+    sent = [0, 0]
+
+    def copier(sender):
+        def copy(source, landing, target, span, arrival):
+            arrival.count += span[1] - span[0]
+            sent[sender] += span[1] - span[0]
+            described(source, landing, target, sender, arrival.index).start()
+
+        return copy
+
+    copy_row, copy_col = copier(0), copier(1)
 
     def row_part(k, first, last):
         return row.at[k, :, pl.ds(first, last - first), :]
@@ -135,30 +178,23 @@
         start = pl.multiple_of(base + first, 16)
         return col.at[k, :, pl.ds(start, last - first), :]
 
-    rows = Gather(copy, row_part, x, y_lo, right, left)
-    cols = Gather(copy, col_part, z, y_hi, up, down)
+    rows = Gather(copy_row, Arrival, row_part, x, y_lo, right, left)
+    cols = Gather(copy_col, Arrival, col_part, z, y_hi, up, down)
     both = (rows, cols)
-    shared = []
-
-    def share(offset, other, span):
-        piece = cols.piece(offset, other, span)
-        shared.append(copy(piece, piece, sibling))
-
-    def wait_shared():
-        for made in shared:
-            made.wait_recv()
-        shared.clear()
-
-    crossed, turned = {}, {}
+    crossed = [Arrival() for _ in CHUNKS]
+    turned = [Arrival() for _ in CHUNKS]
+    shared = [Arrival() for _ in range(4)]
+
+    def share(stage, offset, other, span):
+        cols.move(offset, other, span, sibling, shared[stage])
 
     def cross(c):
-        piece = rows.piece(0, False, CHUNKS[c])
-        crossed[c] = copy(piece, piece, beside)
+        rows.move(0, False, CHUNKS[c], beside, crossed[c])
 
     def turn(c):
-        crossed[c].wait_recv()
+        crossed[c].wait()
         landing = col_part(col_own, *CHUNKS[c])
-        turned[c] = copy(rows.piece(0, True, CHUNKS[c]), landing, opposite)
+        copy_row(rows.piece(0, True, CHUNKS[c]), landing, opposite, CHUNKS[c], turned[c])
 
     def kind_of(place, low, k):
         distance = (k // 2 - place + 4) % 4
@@ -252,15 +288,15 @@
             g.send_behind(False, second)
         cross(first)
         cross(second)
-    share(0, False, WHOLE)
+    share(0, 0, False, WHOLE)
     acc[...] = jnp.zeros_like(acc)
 
     for first, second in ((0, 3), (1, 2)):
         for g in both:
-            g.from_behind[False, first].wait_recv()
-            g.pass_ahead(False, first, CHUNKS[first])
-            g.from_ahead[False, second].wait_recv()
-            g.pass_behind(False, second, CHUNKS[second])
+            g.from_behind[False, first].wait()
+            g.pass_ahead(first)
+            g.from_ahead[False, second].wait()
+            g.pass_behind(second)
         if first == 0:
             turn(0)
     for first, second in ((2, 1), (3, 0)):
@@ -273,86 +309,68 @@
     for c in range(3):
         rows.send_ahead(True, c)
         rows.send_behind(True, 3 - c)
-    far = {}
     for first, second in ((0, 3), (1, 2)):
-        for g in both:
-            g.far_from_behind[False, first].wait_recv()
-            g.far_from_ahead[False, second].wait_recv()
-    for span in (MIDDLE, UPPER):
         for g, target in ((rows, beside), (cols, across)):
-            piece = g.piece(2, False, span)
-            far[g, span] = copy(piece, piece, target)
-    share(2, False, WHOLE)
-    turned[0].wait_recv()
+            g.far[first].wait()
+            g.cross_far(first, target)
+            g.cross_far(second, target)
+    share(0, 2, False, WHOLE)
+    turned[0].wait()
     cols.send_ahead(True, 0)
-    turned[3].wait_recv()
+    turned[3].wait()
     cols.send_behind(True, 3)
-    turned[1].wait_recv()
+    turned[1].wait()
     cols.send_ahead(True, 1)
-    turned[2].wait_recv()
+    turned[2].wait()
     cols.send_ahead(True, 2)
     cols.send_behind(True, 2)
     cols.send_behind(True, 1)
-    share(0, True, WHOLE)
-    for first, second in ((2, 1), (3, 0)):
-        for g in both:
-            g.from_behind[False, first].wait_recv()
-            g.from_ahead[False, second].wait_recv()
-    share(3, False, WHOLE)
-    share(1, False, WHOLE)
+    share(0, 0, True, WHOLE)
     for g in both:
-        g.from_behind[True, 0].wait_recv()
-        g.pass_ahead(True, 0, LOW)
-        g.send_ahead(True, 3)
-        g.from_ahead[True, 3].wait_recv()
-        g.pass_behind(True, 3, HIGH)
-        g.send_behind(True, 0)
-    wait_shared()
+        g.from_behind[False, 3].wait()
+    share(0, 3, False, WHOLE)
+    share(0, 1, False, WHOLE)
+    for g in both:
+        g.pass_edges()
+    shared[0].wait()
     over_blocks(multiply_early)
 
-    for g in (cols, rows):
-        for c in (1, 2):
-            g.from_behind[True, c].wait_recv()
-            g.from_ahead[True, 3 - c].wait_recv()
-        if g is cols:
-            share(3, True, (0, ROWS - TAIL))
-            share(1, True, (TAIL, ROWS))
-    wait_shared()
+    cols.from_behind[True, 1].wait()
+    share(1, 3, True, (0, ROWS - TAIL))
+    share(1, 1, True, (TAIL, ROWS))
+    rows.from_behind[True, 1].wait()
+    shared[1].wait()
     over_blocks(multiply_first(0, 0))
 
-    for span in (MIDDLE, UPPER):
-        far[cols, span].wait_recv()
-        share(2, True, span)
-    cols.far_from_behind[True, 0].wait_recv()
-    share(2, True, LOW)
-    cols.far_from_ahead[True, 3].wait_recv()
-    share(2, True, HIGH)
-    for span in (MIDDLE, UPPER):
-        far[rows, span].wait_recv()
-    rows.far_from_behind[True, 0].wait_recv()
-    rows.far_from_ahead[True, 3].wait_recv()
-    wait_shared()
+    cols.far_crossed.wait()
+    share(2, 2, True, (LOW[1], HIGH[0]))
+    cols.far_passed.wait()
+    share(2, 2, True, LOW)
+    share(2, 2, True, HIGH)
+    rows.far_crossed.wait()
+    rows.far_passed.wait()
+    shared[2].wait()
     over_blocks(multiply_first(2, 2))
 
-    cols.from_behind[True, 3].wait_recv()
-    share(3, True, CHUNKS[3])
-    cols.from_ahead[True, 0].wait_recv()
-    share(1, True, CHUNKS[0])
-    rows.from_behind[True, 3].wait_recv()
-    rows.from_ahead[True, 0].wait_recv()
+    cols.from_behind[True, 3].wait()
+    share(3, 3, True, CHUNKS[3])
+    share(3, 1, True, CHUNKS[0])
+    rows.from_behind[True, 3].wait()
     over_blocks(multiply_last_rows)
-    wait_shared()
+    shared[3].wait()
     over_blocks(multiply_last)
 
     mask = spread(pats[2])
     for i in range(BLOCK_ROWS):
         block_rows = pl.ds(i * BLOCK, BLOCK)
         out[block_rows, :] = acc[block_rows, :] * mask[i : i + 1, :]
-    for made in started:
-        made.wait_send()
-
-
-def shards(hamiltonian, density, h_pattern, p_pattern, keep_mask):
+    for sender, count in enumerate(sent):
+        area = extent(count)
+        described(area, area, sibling, sender, 0).wait_send()
+
+
+def shards(*arrays):
+    arrays = [pltpu.with_memory_space_constraint(array, pltpu.HBM) for array in arrays]
     return pl.pallas_call(
         kernel,
         out_shape=jax.ShapeDtypeStruct((ROWS, COLS), jnp.float32),
@@ -364,15 +382,15 @@
             pltpu.VMEM((ROWS, COLS), jnp.float32),
             pltpu.VMEM((2, ROWS, COLS), jnp.bfloat16),
             pltpu.VMEM((3, BLOCK_ROWS, BLOCK_COLS), jnp.int32),
-            pltpu.SemaphoreType.DMA((COPIES,)),
-            pltpu.SemaphoreType.DMA((COPIES,)),
+            pltpu.SemaphoreType.DMA((2,)),
+            pltpu.SemaphoreType.DMA((ARRIVALS,)),
             pltpu.SemaphoreType.DMA((5,)),
         ],
         compiler_params=pltpu.CompilerParams(
-            collective_id=0, has_side_effects=True, vmem_limit_bytes=60 * 1024 * 1024
+            collective_id=0, has_side_effects=True, vmem_limit_bytes=48 * 1024 * 1024
         ),
         name="commutator",
-    )(hamiltonian, density, h_pattern, p_pattern, keep_mask)
+    )(*arrays)
 
 
 def solution(mesh):

time: 85.5 us -> 81.6 us (0.954)
  Pallas kernels: 82.9 us -> 80.5 us
  local copies, waits for them, and re-layouts: 2.36 us -> 1.02 us
    pallas_call x1, Pallas kernels: 82.9 us -> 80.5 us  [shards(): pl.pallas_call(kernel, out_shape=jax.ShapeDtypeStruct((ROWS, COLS), jnp.f...]
    unnamed x1, local copies, waits for them, and re-layouts: 2.36 us -> 1.02 us
where the time goes in v5:
time: 81.6 us; the launch traced here: 81.5 us
  Pallas kernels  80.5 us (99%)
  local copies, waits for them, and re-layouts  1.02 us (1%)
    pallas_call x1, Pallas kernels, shards(): pl.pallas_call(kernel, out_shape=jax.ShapeDtypeStruct((ROWS, COLS), jnp.f...  80.5 us

profile of v5, /device:TPU:1, one launch (start us, length us, event | category | flops | bytes accessed | tf_op | source)
XLA Modules:
  0.0 81.5 jit_solution(254643475661071092)
XLA Ops:
  0.0 80.5 %commutator.1 = f32[384,768]{1,0:T(8,128)S(1)} custom-call(bf16[384,768]{1,0:T(8,128)(2,1)} %ham.1, bf16[384,768]{1,0:T(8,128)(2,1)} %den.1, s32[6,12]{1,0:T(8,128)} %h_pat.1, s32[6,12]{1,0:T(8,128)} %p_pat.1, s32[6,12]{1,0:T(8,128)} %keep.1), custom_call_target="tpu_custom_call" | custom-call | tf_op jit(solution)/shard_map/commutator/pallas_call | solution.py:374
  80.5 1.0 %copy.7 = f32[384,768]{1,0:T(8,128)} copy(f32[384,768]{1,0:T(8,128)S(1)} %commutator.1) | data formatting | bytes 2359296

commit v6 on v5

--- a/solution.py
+++ b/solution.py
@@ -1,3 +1,5 @@
+import functools
+
 import jax
 import jax.numpy as jnp
 from jax import lax
@@ -14,11 +16,11 @@
 CUTS = (0, 128, 192, 256, 384)
 CHUNKS = tuple(zip(CUTS[:-1], CUTS[1:]))
 WHOLE = (0, ROWS)
-LOW = (0, 64)
-MIDDLE = ((64, 128), (128, 192), (192, 256), (256, 320))
-HIGH = (320, 384)
+EDGE = 48
+LOW_EDGE = (ROWS - 2 * EDGE, ROWS - EDGE)
+HIGH_EDGE = (ROWS - EDGE, ROWS)
 TAIL = 128
-ARRIVALS = 38
+ARRIVALS = 39
 
 
 def device_of(x, y, z, core):
@@ -33,18 +35,18 @@
 
 
 class Gather:
-    def __init__(self, copy, arrival, part, place, low, ahead, behind):
+    def __init__(self, copy, arrival, part, place, low, ahead, behind, crossed):
         self.copy, self.part, self.place, self.low = copy, part, place, low
-        self.ahead, self.behind = ahead, behind
+        self.ahead, self.behind, self.crossed = ahead, behind, crossed
         first, second, third, fourth, last = (arrival() for _ in range(5))
         self.from_behind = {(False, 0): first, (False, 1): second, (False, 2): last, (False, 3): last}
         self.from_ahead = {(False, 3): third, (False, 2): fourth, (False, 1): last, (False, 0): last}
         first, second, middle, last = (arrival() for _ in range(4))
-        self.from_behind.update({(True, 0): first, (True, 1): middle, (True, 2): middle, (True, 3): last})
-        self.from_ahead.update({(True, 3): second, (True, 2): middle, (True, 1): middle, (True, 0): last})
+        self.from_behind.update({(True, 3): first, (True, 1): middle, (True, 2): middle, (True, 0): last})
+        self.from_ahead.update({(True, 3): second, (True, 1): middle, (True, 2): middle, (True, 0): last})
         outer, inner = arrival(), arrival()
         self.far = {0: outer, 3: outer, 1: inner, 2: inner}
-        self.far_passed, self.far_crossed = arrival(), arrival()
+        self.far_crossed, self.far_edges = arrival(), arrival()
 
     def k(self, offset, other):
         low = 1 - self.low if other else self.low
@@ -70,15 +72,15 @@
         self.move(1, False, CHUNKS[c], self.behind, self.far[c])
 
     def pass_edges(self):
-        self.from_behind[True, 0].wait()
-        self.move(3, True, LOW, self.ahead, self.far_passed)
-        self.send_ahead(True, 3)
+        self.from_behind[True, 3].wait()
+        self.move(3, True, LOW_EDGE, self.ahead, self.far_edges)
         self.from_ahead[True, 3].wait()
-        self.move(1, True, HIGH, self.behind, self.far_passed)
-        self.send_behind(True, 0)
+        self.move(1, True, HIGH_EDGE, self.behind, self.far_edges)
 
     def cross_far(self, c, target):
-        self.move(2, False, MIDDLE[c], target, self.far_crossed)
+        span = (CHUNKS[c][0], min(CHUNKS[c][1], LOW_EDGE[0]))
+        arrival = self.far_crossed if c in self.crossed else self.far_edges
+        self.move(2, False, span, target, arrival)
 
 
 def kernel(ham, den, h_pat, p_pat, keep, out, row, col, acc, tiles, pats, send, recv, load):
@@ -178,12 +180,12 @@
         start = pl.multiple_of(base + first, 16)
         return col.at[k, :, pl.ds(start, last - first), :]
 
-    rows = Gather(copy_row, Arrival, row_part, x, y_lo, right, left)
-    cols = Gather(copy_col, Arrival, col_part, z, y_hi, up, down)
+    rows = Gather(copy_row, Arrival, row_part, x, y_lo, right, left, (0, 1, 2))
+    cols = Gather(copy_col, Arrival, col_part, z, y_hi, up, down, (0,))
     both = (rows, cols)
     crossed = [Arrival() for _ in CHUNKS]
     turned = [Arrival() for _ in CHUNKS]
-    shared = [Arrival() for _ in range(4)]
+    shared = [Arrival() for _ in range(5)]
 
     def share(stage, offset, other, span):
         cols.move(offset, other, span, sibling, shared[stage])
@@ -202,92 +204,50 @@
         late = jnp.where(distance == 2, 2, 1)
         return jnp.where((other == 0) | (distance == 0), 0, late)
 
-    def offset_of(place, k):
-        behind = (k // 2 - place + 4) % 4 == 3
-        return jnp.where(behind, 0, TAIL), jnp.where(behind, ROWS - TAIL, 0)
-
-    def product(k, first, count, inner, depth):
-        out_rows = pl.ds(pl.multiple_of(first, TAIL), count)
+    def product(k, out_part, inner_part):
+        out_span = slice(*out_part)
+        if inner_part == WHOLE:
+            inner_spans = [slice(None)]
+        else:
+            inner_spans = [slice(base + inner_part[0], base + inner_part[1]) for base in (0, ROWS)]
 
         def left(matrix):
-            if depth == ROWS:
-                return row[k, matrix, out_rows, :]
-            spans = [pl.ds(pl.multiple_of(i * ROWS + inner, TAIL), depth) for i in range(2)]
-            return jnp.concatenate([row[k, matrix, out_rows, span] for span in spans], axis=1)
+            pieces = [row[k, matrix, out_span, inner] for inner in inner_spans]
+            return jnp.concatenate(pieces, axis=1)
 
         def right(matrix):
-            if depth == ROWS:
-                return col[k, matrix]
-            spans = [pl.ds(pl.multiple_of(i * ROWS + inner, TAIL), depth) for i in range(2)]
-            return jnp.concatenate([col[k, matrix, span, :] for span in spans], axis=0)
+            return jnp.concatenate([col[k, matrix, inner, :] for inner in inner_spans], axis=0)
 
         forward = jnp.dot(left(0), right(1), preferred_element_type=jnp.float32)
         backward = jnp.dot(left(1), right(0), preferred_element_type=jnp.float32)
-        acc[out_rows, :] += forward - backward
-
-    def over_blocks(body):
+        acc[out_span, :] += forward - backward
+
+    def stage(*entries):
         @pl.loop(0, 8)
         def _(k):
-            body(k, kind_of(x, y_lo, k), kind_of(z, y_hi, k))
-
-    def multiply_early(k, r, c):
-        @pl.when((r == 0) & (c == 0))
-        def _():
-            product(k, 0, ROWS, 0, ROWS)
-
-    def multiply_first(row_other, col_other):
-        def body(k, r, c):
-            row_start, _ = offset_of(x, k)
-            col_start, _ = offset_of(z, k)
-
-            @pl.when((r == 1) & (c == col_other))
-            def _():
-                product(k, row_start, ROWS - TAIL, 0, ROWS)
-
-            @pl.when((r == row_other) & (c == 1))
-            def _():
-                product(k, 0, ROWS, col_start, ROWS - TAIL)
-
-            if row_other == 0:
-
-                @pl.when((r == 1) & (c == 1))
+            r, c = kind_of(x, y_lo, k), kind_of(z, y_hi, k)
+            for row_kinds, col_kinds, *parts in entries:
+                row_fits = functools.reduce(jnp.logical_or, [r == kind for kind in row_kinds])
+                col_fits = functools.reduce(jnp.logical_or, [c == kind for kind in col_kinds])
+
+                @pl.when(row_fits & col_fits)
                 def _():
-                    product(k, row_start, ROWS - TAIL, col_start, ROWS - TAIL)
-
-            else:
-
-                @pl.when(((r == 2) & (c != 1)) | ((r != 1) & (c == 2)))
-                def _():
-                    product(k, 0, ROWS, 0, ROWS)
-
-        return body
-
-    def multiply_last_rows(k, r, c):
-        _, row_start = offset_of(x, k)
-
-        @pl.when((r == 1) & (c != 1))
-        def _():
-            product(k, row_start, TAIL, 0, ROWS)
-
-    def multiply_last(k, r, c):
-        row_first, row_start = offset_of(x, k)
-        _, col_start = offset_of(z, k)
-
-        @pl.when((r == 1) & (c == 1))
-        def _():
-            product(k, row_start, TAIL, 0, ROWS)
-            product(k, row_first, ROWS - TAIL, col_start, TAIL)
-
-        @pl.when((r != 1) & (c == 1))
-        def _():
-            product(k, 0, ROWS, col_start, TAIL)
+                    for out_part, inner_part in parts:
+                        product(k, out_part, inner_part)
+
+    near_first, near_last = (TAIL, ROWS), (0, TAIL)
+    far_rows_first, far_rows_last = (0, 2 * TAIL), (2 * TAIL, ROWS)
+    far_cols_first, far_cols_last = (0, TAIL), (TAIL, ROWS)
 
     for first, second in ((0, 3), (1, 2)):
         for g in both:
             g.send_ahead(False, first)
             g.send_behind(False, second)
-        cross(first)
-        cross(second)
+        if first == 0:
+            cross(3)
+            cross(1)
+    cross(2)
+    cross(0)
     share(0, 0, False, WHOLE)
     acc[...] = jnp.zeros_like(acc)
 
@@ -298,34 +258,32 @@
             g.from_ahead[False, second].wait()
             g.pass_behind(second)
         if first == 0:
-            turn(0)
+            turn(3)
     for first, second in ((2, 1), (3, 0)):
         for g in both:
             g.send_ahead(False, first)
             g.send_behind(False, second)
-    for c in (3, 1, 2):
-        turn(c)
-
-    for c in range(3):
+    turn(1)
+    turn(2)
+
+    def cross_far(g, target, *chunks):
+        for c in chunks:
+            g.far[c].wait()
+            g.cross_far(c, target)
+
+    cross_far(rows, beside, 0)
+    turn(0)
+    for c in (3, 1, 2, 0):
         rows.send_ahead(True, c)
-        rows.send_behind(True, 3 - c)
-    for first, second in ((0, 3), (1, 2)):
-        for g, target in ((rows, beside), (cols, across)):
-            g.far[first].wait()
-            g.cross_far(first, target)
-            g.cross_far(second, target)
+        rows.send_behind(True, c)
+    cross_far(rows, beside, 1, 2, 3)
+    for c in (3, 1, 2, 0):
+        turned[c].wait()
+        cols.send_ahead(True, c)
+        cols.send_behind(True, c)
+    share(0, 0, True, WHOLE)
+    cross_far(cols, across, 0, 1, 2, 3)
     share(0, 2, False, WHOLE)
-    turned[0].wait()
-    cols.send_ahead(True, 0)
-    turned[3].wait()
-    cols.send_behind(True, 3)
-    turned[1].wait()
-    cols.send_ahead(True, 1)
-    turned[2].wait()
-    cols.send_ahead(True, 2)
-    cols.send_behind(True, 2)
-    cols.send_behind(True, 1)
-    share(0, 0, True, WHOLE)
     for g in both:
         g.from_behind[False, 3].wait()
     share(0, 3, False, WHOLE)
@@ -333,32 +291,53 @@
     for g in both:
         g.pass_edges()
     shared[0].wait()
-    over_blocks(multiply_early)
+    stage(((0,), (0,), (WHOLE, WHOLE)))
+
+    rows.far_crossed.wait()
+    stage(((2,), (0,), (far_rows_first, WHOLE)))
 
     cols.from_behind[True, 1].wait()
-    share(1, 3, True, (0, ROWS - TAIL))
-    share(1, 1, True, (TAIL, ROWS))
+    share(1, 3, True, near_first)
+    share(1, 1, True, near_first)
+    cols.far_crossed.wait()
+    share(2, 2, True, far_cols_first)
     rows.from_behind[True, 1].wait()
     shared[1].wait()
-    over_blocks(multiply_first(0, 0))
-
-    cols.far_crossed.wait()
-    share(2, 2, True, (LOW[1], HIGH[0]))
-    cols.far_passed.wait()
-    share(2, 2, True, LOW)
-    share(2, 2, True, HIGH)
-    rows.far_crossed.wait()
-    rows.far_passed.wait()
     shared[2].wait()
-    over_blocks(multiply_first(2, 2))
-
-    cols.from_behind[True, 3].wait()
-    share(3, 3, True, CHUNKS[3])
-    share(3, 1, True, CHUNKS[0])
-    rows.from_behind[True, 3].wait()
-    over_blocks(multiply_last_rows)
+    stage(
+        ((1,), (0,), (near_first, WHOLE)),
+        ((0,), (1,), (WHOLE, near_first)),
+        ((1,), (1,), (near_first, near_first)),
+        ((2,), (1,), (far_rows_first, near_first)),
+        ((0,), (2,), (WHOLE, far_cols_first)),
+        ((1,), (2,), (near_first, far_cols_first)),
+        ((2,), (2,), (far_rows_first, far_cols_first)),
+    )
+
+    cols.from_behind[True, 0].wait()
+    share(3, 3, True, near_last)
+    share(3, 1, True, near_last)
+    rows.from_behind[True, 0].wait()
+    stage(
+        ((1,), (0,), (near_last, WHOLE)),
+        ((1,), (2,), (near_last, far_cols_first)),
+    )
     shared[3].wait()
-    over_blocks(multiply_last)
+    stage(
+        ((0,), (1,), (WHOLE, near_last)),
+        ((1,), (1,), (near_last, WHOLE), (near_first, near_last)),
+        ((2,), (1,), (far_rows_first, near_last)),
+    )
+
+    cols.far_edges.wait()
+    share(4, 2, True, far_cols_last)
+    rows.far_edges.wait()
+    stage(((2,), (0, 1), (far_rows_last, WHOLE)))
+    shared[4].wait()
+    stage(
+        ((0, 1), (2,), (WHOLE, far_cols_last)),
+        ((2,), (2,), (far_rows_last, WHOLE), (far_rows_first, far_cols_last)),
+    )
 
     mask = spread(pats[2])
     for i in range(BLOCK_ROWS):

time: 81.6 us -> 80.5 us (0.987)
  Pallas kernels: 80.5 us -> 79.3 us
    pallas_call x1, Pallas kernels: 80.5 us -> 79.3 us  [shards(): pl.pallas_call(kernel, out_shape=jax.ShapeDtypeStruct((ROWS, COLS), jnp.f...]
where the time goes in v6:
time: 80.5 us; the launch traced here: 80.3 us
  Pallas kernels  79.3 us (99%)
  local copies, waits for them, and re-layouts  1.02 us (1%)
    pallas_call x1, Pallas kernels, shards(): pl.pallas_call(kernel, out_shape=jax.ShapeDtypeStruct((ROWS, COLS), jnp.f...  79.3 us

profile of v6, /device:TPU:1, one launch (start us, length us, event | category | flops | bytes accessed | tf_op | source)
XLA Modules:
  0.0 80.3 jit_solution(13934397617179656890)
XLA Ops:
  0.0 79.3 %commutator.1 = f32[384,768]{1,0:T(8,128)S(1)} custom-call(bf16[384,768]{1,0:T(8,128)(2,1)} %ham.1, bf16[384,768]{1,0:T(8,128)(2,1)} %den.1, s32[6,12]{1,0:T(8,128)} %h_pat.1, s32[6,12]{1,0:T(8,128)} %p_pat.1, s32[6,12]{1,0:T(8,128)} %keep.1), custom_call_target="tpu_custom_call" | custom-call | tf_op jit(solution)/shard_map/commutator/pallas_call | solution.py:353
  79.3 1.0 %copy.7 = f32[384,768]{1,0:T(8,128)} copy(f32[384,768]{1,0:T(8,128)S(1)} %commutator.1) | data formatting | bytes 2359296

commit v7 on v6

--- a/solution.py
+++ b/solution.py
@@ -16,9 +16,8 @@
 CUTS = (0, 128, 192, 256, 384)
 CHUNKS = tuple(zip(CUTS[:-1], CUTS[1:]))
 WHOLE = (0, ROWS)
-EDGE = 48
-LOW_EDGE = (ROWS - 2 * EDGE, ROWS - EDGE)
-HIGH_EDGE = (ROWS - EDGE, ROWS)
+ROW_EDGE = 64
+COL_EDGE = 32
 TAIL = 128
 ARRIVALS = 39
 
@@ -35,9 +34,11 @@
 
 
 class Gather:
-    def __init__(self, copy, arrival, part, place, low, ahead, behind, crossed):
+    def __init__(self, copy, arrival, part, place, low, ahead, behind, crossed, edge):
         self.copy, self.part, self.place, self.low = copy, part, place, low
         self.ahead, self.behind, self.crossed = ahead, behind, crossed
+        self.low_edge = (ROWS - 2 * edge, ROWS - edge)
+        self.high_edge = (ROWS - edge, ROWS)
         first, second, third, fourth, last = (arrival() for _ in range(5))
         self.from_behind = {(False, 0): first, (False, 1): second, (False, 2): last, (False, 3): last}
         self.from_ahead = {(False, 3): third, (False, 2): fourth, (False, 1): last, (False, 0): last}
@@ -73,17 +74,19 @@
 
     def pass_edges(self):
         self.from_behind[True, 3].wait()
-        self.move(3, True, LOW_EDGE, self.ahead, self.far_edges)
+        self.move(3, True, self.low_edge, self.ahead, self.far_edges)
         self.from_ahead[True, 3].wait()
-        self.move(1, True, HIGH_EDGE, self.behind, self.far_edges)
+        self.move(1, True, self.high_edge, self.behind, self.far_edges)
 
     def cross_far(self, c, target):
-        span = (CHUNKS[c][0], min(CHUNKS[c][1], LOW_EDGE[0]))
+        span = (CHUNKS[c][0], min(CHUNKS[c][1], self.low_edge[0]))
+        if span[0] == span[1]:
+            return
         arrival = self.far_crossed if c in self.crossed else self.far_edges
         self.move(2, False, span, target, arrival)
 
 
-def kernel(ham, den, h_pat, p_pat, keep, out, row, col, acc, tiles, pats, send, recv, load):
+def kernel(ham, den, h_pat, p_pat, keep, out, row, col, acc, kept, tiles, pats, send, recv, load):
     row_index = lax.axis_index("row")
     col_index = lax.axis_index("col")
     x, y_lo = col_index // 2, col_index % 2
@@ -180,8 +183,8 @@
         start = pl.multiple_of(base + first, 16)
         return col.at[k, :, pl.ds(start, last - first), :]
 
-    rows = Gather(copy_row, Arrival, row_part, x, y_lo, right, left, (0, 1, 2))
-    cols = Gather(copy_col, Arrival, col_part, z, y_hi, up, down, (0,))
+    rows = Gather(copy_row, Arrival, row_part, x, y_lo, right, left, (0, 1, 2), ROW_EDGE)
+    cols = Gather(copy_col, Arrival, col_part, z, y_hi, up, down, (0,), COL_EDGE)
     both = (rows, cols)
     crossed = [Arrival() for _ in CHUNKS]
     turned = [Arrival() for _ in CHUNKS]
@@ -250,6 +253,7 @@
     cross(0)
     share(0, 0, False, WHOLE)
     acc[...] = jnp.zeros_like(acc)
+    kept[...] = spread(pats[2])
 
     for first, second in ((0, 3), (1, 2)):
         for g in both:
@@ -273,7 +277,7 @@
 
     cross_far(rows, beside, 0)
     turn(0)
-    for c in (3, 1, 2, 0):
+    for c in (3, 1, 2):
         rows.send_ahead(True, c)
         rows.send_behind(True, c)
     cross_far(rows, beside, 1, 2, 3)
@@ -288,8 +292,10 @@
         g.from_behind[False, 3].wait()
     share(0, 3, False, WHOLE)
     share(0, 1, False, WHOLE)
-    for g in both:
-        g.pass_edges()
+    rows.pass_edges()
+    rows.send_ahead(True, 0)
+    rows.send_behind(True, 0)
+    cols.pass_edges()
     shared[0].wait()
     stage(((0,), (0,), (WHOLE, WHOLE)))
 
@@ -314,35 +320,35 @@
         ((2,), (2,), (far_rows_first, far_cols_first)),
     )
 
+    rows.far_edges.wait()
+    stage(
+        ((2,), (0,), (far_rows_last, WHOLE)),
+        ((2,), (1,), (far_rows_last, near_first)),
+        ((2,), (2,), (far_rows_last, far_cols_first)),
+    )
+
     cols.from_behind[True, 0].wait()
     share(3, 3, True, near_last)
     share(3, 1, True, near_last)
+    shared[3].wait()
+    stage(
+        ((0, 2), (1,), (WHOLE, near_last)),
+        ((1,), (1,), (near_first, near_last)),
+    )
+
+    cols.far_edges.wait()
+    share(4, 2, True, far_cols_last)
     rows.from_behind[True, 0].wait()
     stage(
-        ((1,), (0,), (near_last, WHOLE)),
+        ((1,), (0, 1), (near_last, WHOLE)),
         ((1,), (2,), (near_last, far_cols_first)),
     )
-    shared[3].wait()
-    stage(
-        ((0,), (1,), (WHOLE, near_last)),
-        ((1,), (1,), (near_last, WHOLE), (near_first, near_last)),
-        ((2,), (1,), (far_rows_first, near_last)),
-    )
-
-    cols.far_edges.wait()
-    share(4, 2, True, far_cols_last)
-    rows.far_edges.wait()
-    stage(((2,), (0, 1), (far_rows_last, WHOLE)))
     shared[4].wait()
-    stage(
-        ((0, 1), (2,), (WHOLE, far_cols_last)),
-        ((2,), (2,), (far_rows_last, WHOLE), (far_rows_first, far_cols_last)),
-    )
-
-    mask = spread(pats[2])
+    stage(((0, 1, 2), (2,), (WHOLE, far_cols_last)))
+
     for i in range(BLOCK_ROWS):
         block_rows = pl.ds(i * BLOCK, BLOCK)
-        out[block_rows, :] = acc[block_rows, :] * mask[i : i + 1, :]
+        out[block_rows, :] = acc[block_rows, :] * kept[i : i + 1, :]
     for sender, count in enumerate(sent):
         area = extent(count)
         described(area, area, sibling, sender, 0).wait_send()
@@ -359,6 +365,7 @@
             pltpu.VMEM((8, 2, ROWS, COLS), jnp.bfloat16),
             pltpu.VMEM((8, 2, 2 * ROWS, COLS), jnp.bfloat16),
             pltpu.VMEM((ROWS, COLS), jnp.float32),
+            pltpu.VMEM((BLOCK_ROWS, COLS), jnp.float32),
             pltpu.VMEM((2, ROWS, COLS), jnp.bfloat16),
             pltpu.VMEM((3, BLOCK_ROWS, BLOCK_COLS), jnp.int32),
             pltpu.SemaphoreType.DMA((2,)),

time: 80.5 us -> 80 us (level)
  no operation moved by 1% of the time
where the time goes in v7:
time: 80 us; the launch traced here: 79.9 us
  Pallas kernels  78.9 us (99%)
  local copies, waits for them, and re-layouts  1.02 us (1%)
    pallas_call x1, Pallas kernels, shards(): pl.pallas_call(kernel, out_shape=jax.ShapeDtypeStruct((ROWS, COLS), jnp.f...  78.9 us

profile of v7, /device:TPU:1, one launch (start us, length us, event | category | flops | bytes accessed | tf_op | source)
XLA Modules:
  0.0 79.9 jit_solution(4402865723506007876)
XLA Ops:
  0.0 78.9 %commutator.1 = f32[384,768]{1,0:T(8,128)S(1)} custom-call(bf16[384,768]{1,0:T(8,128)(2,1)} %ham.1, bf16[384,768]{1,0:T(8,128)(2,1)} %den.1, s32[6,12]{1,0:T(8,128)} %h_pat.1, s32[6,12]{1,0:T(8,128)} %p_pat.1, s32[6,12]{1,0:T(8,128)} %keep.1), custom_call_target="tpu_custom_call" | custom-call | tf_op jit(solution)/shard_map/commutator/pallas_call | solution.py:359
  78.9 1.0 %copy.7 = f32[384,768]{1,0:T(8,128)} copy(f32[384,768]{1,0:T(8,128)S(1)} %commutator.1) | data formatting | bytes 2359296

commit v8 on v7

--- a/solution.py
+++ b/solution.py
@@ -225,18 +225,35 @@
         backward = jnp.dot(left(1), right(0), preferred_element_type=jnp.float32)
         acc[out_span, :] += forward - backward
 
+    def visit(k, r, c, entries):
+        for row_kinds, col_kinds, *parts in entries:
+            fits = [(r == kind) & (c == other) for kind in row_kinds for other in col_kinds]
+
+            @pl.when(functools.reduce(jnp.logical_or, fits))
+            def _():
+                for out_part, inner_part in parts:
+                    product(k, out_part, inner_part)
+
     def stage(*entries):
         @pl.loop(0, 8)
         def _(k):
-            r, c = kind_of(x, y_lo, k), kind_of(z, y_hi, k)
-            for row_kinds, col_kinds, *parts in entries:
-                row_fits = functools.reduce(jnp.logical_or, [r == kind for kind in row_kinds])
-                col_fits = functools.reduce(jnp.logical_or, [c == kind for kind in col_kinds])
-
-                @pl.when(row_fits & col_fits)
-                def _():
-                    for out_part, inner_part in parts:
-                        product(k, out_part, inner_part)
+            visit(k, kind_of(x, y_lo, k), kind_of(z, y_hi, k), entries)
+
+    def stage_of(g, kind, *entries):
+        def body(offset):
+            k = g.k(offset, True)
+            if g is rows:
+                visit(k, kind, kind_of(z, y_hi, k), entries)
+            else:
+                visit(k, kind_of(x, y_lo, k), kind, entries)
+
+        if kind == 2:
+            body(2)
+        else:
+
+            @pl.loop(0, 2)
+            def _(i):
+                body(1 + 2 * i)
 
     near_first, near_last = (TAIL, ROWS), (0, TAIL)
     far_rows_first, far_rows_last = (0, 2 * TAIL), (2 * TAIL, ROWS)
@@ -300,7 +317,7 @@
     stage(((0,), (0,), (WHOLE, WHOLE)))
 
     rows.far_crossed.wait()
-    stage(((2,), (0,), (far_rows_first, WHOLE)))
+    stage_of(rows, 2, ((2,), (0,), (far_rows_first, WHOLE)))
 
     cols.from_behind[True, 1].wait()
     share(1, 3, True, near_first)
@@ -321,7 +338,9 @@
     )
 
     rows.far_edges.wait()
-    stage(
+    stage_of(
+        rows,
+        2,
         ((2,), (0,), (far_rows_last, WHOLE)),
         ((2,), (1,), (far_rows_last, near_first)),
         ((2,), (2,), (far_rows_last, far_cols_first)),
@@ -331,7 +350,9 @@
     share(3, 3, True, near_last)
     share(3, 1, True, near_last)
     shared[3].wait()
-    stage(
+    stage_of(
+        cols,
+        1,
         ((0, 2), (1,), (WHOLE, near_last)),
         ((1,), (1,), (near_first, near_last)),
     )
@@ -339,12 +360,14 @@
     cols.far_edges.wait()
     share(4, 2, True, far_cols_last)
     rows.from_behind[True, 0].wait()
-    stage(
+    stage_of(
+        rows,
+        1,
         ((1,), (0, 1), (near_last, WHOLE)),
         ((1,), (2,), (near_last, far_cols_first)),
     )
     shared[4].wait()
-    stage(((0, 1, 2), (2,), (WHOLE, far_cols_last)))
+    product(cols.k(2, True), WHOLE, far_cols_last)
 
     for i in range(BLOCK_ROWS):
         block_rows = pl.ds(i * BLOCK, BLOCK)

time: 80 us -> 79.4 us (level)
  no operation moved by 1% of the time
where the time goes in v8:
time: 79.4 us; the launch traced here: 79.3 us
  Pallas kernels  78.3 us (99%)
  local copies, waits for them, and re-layouts  1.02 us (1%)
    pallas_call x1, Pallas kernels, shards(): pl.pallas_call(kernel, out_shape=jax.ShapeDtypeStruct((ROWS, COLS), jnp.f...  78.3 us

profile of v8, /device:TPU:1, one launch (start us, length us, event | category | flops | bytes accessed | tf_op | source)
XLA Modules:
  0.0 79.3 jit_solution(5232434748193216800)
XLA Ops:
  0.0 78.3 %commutator.1 = f32[384,768]{1,0:T(8,128)S(1)} custom-call(bf16[384,768]{1,0:T(8,128)(2,1)} %ham.1, bf16[384,768]{1,0:T(8,128)(2,1)} %den.1, s32[6,12]{1,0:T(8,128)} %h_pat.1, s32[6,12]{1,0:T(8,128)} %p_pat.1, s32[6,12]{1,0:T(8,128)} %keep.1), custom_call_target="tpu_custom_call" | custom-call | tf_op jit(solution)/shard_map/commutator/pallas_call | solution.py:382
  78.3 1.0 %copy.7 = f32[384,768]{1,0:T(8,128)} copy(f32[384,768]{1,0:T(8,128)S(1)} %commutator.1) | data formatting | bytes 2359296

commit v9 on v8

--- a/solution.py
+++ b/solution.py
@@ -34,9 +34,9 @@
 
 
 class Gather:
-    def __init__(self, copy, arrival, part, place, low, ahead, behind, crossed, edge):
+    def __init__(self, copy, arrival, part, place, low, ahead, behind, edge):
         self.copy, self.part, self.place, self.low = copy, part, place, low
-        self.ahead, self.behind, self.crossed = ahead, behind, crossed
+        self.ahead, self.behind = ahead, behind
         self.low_edge = (ROWS - 2 * edge, ROWS - edge)
         self.high_edge = (ROWS - edge, ROWS)
         first, second, third, fourth, last = (arrival() for _ in range(5))
@@ -66,6 +66,15 @@
     def send_behind(self, other, c):
         self.move(0, other, CHUNKS[c], self.behind, self.from_ahead[other, c])
 
+    def send_second_half(self):
+        self.move(0, False, (CUTS[2], ROWS), self.ahead, self.from_behind[False, 3])
+        self.move(0, False, (0, CUTS[2]), self.behind, self.from_ahead[False, 0])
+
+    def send_middle(self):
+        span = (CUTS[1], CUTS[3])
+        self.move(0, True, span, self.ahead, self.from_behind[True, 1])
+        self.move(0, True, span, self.behind, self.from_ahead[True, 1])
+
     def pass_ahead(self, c):
         self.move(3, False, CHUNKS[c], self.ahead, self.far[c])
 
@@ -78,12 +87,13 @@
         self.from_ahead[True, 3].wait()
         self.move(1, True, self.high_edge, self.behind, self.far_edges)
 
-    def cross_far(self, c, target):
-        span = (CHUNKS[c][0], min(CHUNKS[c][1], self.low_edge[0]))
-        if span[0] == span[1]:
-            return
-        arrival = self.far_crossed if c in self.crossed else self.far_edges
-        self.move(2, False, span, target, arrival)
+    def cross_far_first(self, target):
+        self.far[0].wait()
+        self.move(2, False, CHUNKS[0], target, self.far_crossed)
+
+    def cross_far_rest(self, target, arrival):
+        self.far[1].wait()
+        self.move(2, False, (CUTS[1], self.low_edge[0]), target, arrival)
 
 
 def kernel(ham, den, h_pat, p_pat, keep, out, row, col, acc, kept, tiles, pats, send, recv, load):
@@ -183,8 +193,8 @@
         start = pl.multiple_of(base + first, 16)
         return col.at[k, :, pl.ds(start, last - first), :]
 
-    rows = Gather(copy_row, Arrival, row_part, x, y_lo, right, left, (0, 1, 2), ROW_EDGE)
-    cols = Gather(copy_col, Arrival, col_part, z, y_hi, up, down, (0,), COL_EDGE)
+    rows = Gather(copy_row, Arrival, row_part, x, y_lo, right, left, ROW_EDGE)
+    cols = Gather(copy_col, Arrival, col_part, z, y_hi, up, down, COL_EDGE)
     both = (rows, cols)
     crossed = [Arrival() for _ in CHUNKS]
     turned = [Arrival() for _ in CHUNKS]
@@ -280,31 +290,30 @@
             g.pass_behind(second)
         if first == 0:
             turn(3)
-    for first, second in ((2, 1), (3, 0)):
-        for g in both:
-            g.send_ahead(False, first)
-            g.send_behind(False, second)
+    for g in both:
+        g.send_second_half()
     turn(1)
     turn(2)
 
-    def cross_far(g, target, *chunks):
-        for c in chunks:
-            g.far[c].wait()
-            g.cross_far(c, target)
-
-    cross_far(rows, beside, 0)
+    rows.cross_far_first(beside)
     turn(0)
-    for c in (3, 1, 2):
-        rows.send_ahead(True, c)
-        rows.send_behind(True, c)
-    cross_far(rows, beside, 1, 2, 3)
-    for c in (3, 1, 2, 0):
-        turned[c].wait()
-        cols.send_ahead(True, c)
-        cols.send_behind(True, c)
+    rows.send_ahead(True, 3)
+    rows.send_behind(True, 3)
+    rows.send_middle()
+    rows.cross_far_rest(beside, rows.far_crossed)
+    cols.cross_far_first(across)
+    cols.cross_far_rest(across, cols.far_edges)
+    share(0, 2, False, WHOLE)
+    turned[3].wait()
+    cols.send_ahead(True, 3)
+    cols.send_behind(True, 3)
+    turned[1].wait()
+    turned[2].wait()
+    cols.send_middle()
+    turned[0].wait()
+    cols.send_ahead(True, 0)
+    cols.send_behind(True, 0)
     share(0, 0, True, WHOLE)
-    cross_far(cols, across, 0, 1, 2, 3)
-    share(0, 2, False, WHOLE)
     for g in both:
         g.from_behind[False, 3].wait()
     share(0, 3, False, WHOLE)

time: 79.4 us -> 79.4 us (level)
  no operation moved by 1% of the time
where the time goes in v9:
time: 79.4 us; the launch traced here: 79.3 us
  Pallas kernels  78.3 us (99%)
  local copies, waits for them, and re-layouts  1.02 us (1%)
    pallas_call x1, Pallas kernels, shards(): pl.pallas_call(kernel, out_shape=jax.ShapeDtypeStruct((ROWS, COLS), jnp.f...  78.3 us

profile of v9, /device:TPU:1, one launch (start us, length us, event | category | flops | bytes accessed | tf_op | source)
XLA Modules:
  0.0 79.3 jit_solution(7113794541412677030)
XLA Ops:
  0.0 78.3 %commutator.1 = f32[384,768]{1,0:T(8,128)S(1)} custom-call(bf16[384,768]{1,0:T(8,128)(2,1)} %ham.1, bf16[384,768]{1,0:T(8,128)(2,1)} %den.1, s32[6,12]{1,0:T(8,128)} %h_pat.1, s32[6,12]{1,0:T(8,128)} %p_pat.1, s32[6,12]{1,0:T(8,128)} %keep.1), custom_call_target="tpu_custom_call" | custom-call | tf_op jit(solution)/shard_map/commutator/pallas_call | solution.py:391
  78.3 1.0 %copy.7 = f32[384,768]{1,0:T(8,128)} copy(f32[384,768]{1,0:T(8,128)S(1)} %commutator.1) | data formatting | bytes 2359296

commit v10 on v8

--- a/solution.py
+++ b/solution.py
@@ -19,7 +19,7 @@
 ROW_EDGE = 64
 COL_EDGE = 32
 TAIL = 128
-ARRIVALS = 39
+ARRIVALS = 40
 
 
 def device_of(x, y, z, core):
@@ -188,7 +188,7 @@
     both = (rows, cols)
     crossed = [Arrival() for _ in CHUNKS]
     turned = [Arrival() for _ in CHUNKS]
-    shared = [Arrival() for _ in range(5)]
+    shared = [Arrival() for _ in range(6)]
 
     def share(stage, offset, other, span):
         cols.move(offset, other, span, sibling, shared[stage])
@@ -347,15 +347,20 @@
     )
 
     cols.from_behind[True, 0].wait()
-    share(3, 3, True, near_last)
     share(3, 1, True, near_last)
-    shared[3].wait()
-    stage_of(
-        cols,
-        1,
-        ((0, 2), (1,), (WHOLE, near_last)),
-        ((1,), (1,), (near_first, near_last)),
-    )
+    share(5, 3, True, near_last)
+    for arrived, offset in ((3, 1), (5, 3)):
+        shared[arrived].wait()
+        k = cols.k(offset, True)
+        visit(
+            k,
+            kind_of(x, y_lo, k),
+            1,
+            (
+                ((0, 2), (1,), (WHOLE, near_last)),
+                ((1,), (1,), (near_first, near_last)),
+            ),
+        )
 
     cols.far_edges.wait()
     share(4, 2, True, far_cols_last)

time: 79.4 us -> 79 us (level)
  no operation moved by 1% of the time
where the time goes in v10:
time: 79 us; the launch traced here: 78.9 us
  Pallas kernels  77.9 us (99%)
  local copies, waits for them, and re-layouts  1.02 us (1%)
    pallas_call x1, Pallas kernels, shards(): pl.pallas_call(kernel, out_shape=jax.ShapeDtypeStruct((ROWS, COLS), jnp.f...  77.9 us

profile of v10, /device:TPU:1, one launch (start us, length us, event | category | flops | bytes accessed | tf_op | source)
XLA Modules:
  0.0 78.9 jit_solution(17965735126368890571)
XLA Ops:
  0.0 77.9 %commutator.1 = f32[384,768]{1,0:T(8,128)S(1)} custom-call(bf16[384,768]{1,0:T(8,128)(2,1)} %ham.1, bf16[384,768]{1,0:T(8,128)(2,1)} %den.1, s32[6,12]{1,0:T(8,128)} %h_pat.1, s32[6,12]{1,0:T(8,128)} %p_pat.1, s32[6,12]{1,0:T(8,128)} %keep.1), custom_call_target="tpu_custom_call" | custom-call | tf_op jit(solution)/shard_map/commutator/pallas_call | solution.py:387
  77.9 1.0 %copy.7 = f32[384,768]{1,0:T(8,128)} copy(f32[384,768]{1,0:T(8,128)S(1)} %commutator.1) | data formatting | bytes 2359296

commit v11 on v10

--- a/solution.py
+++ b/solution.py
@@ -19,7 +19,7 @@
 ROW_EDGE = 64
 COL_EDGE = 32
 TAIL = 128
-ARRIVALS = 40
+ARRIVALS = 43
 
 
 def device_of(x, y, z, core):
@@ -47,7 +47,7 @@
         self.from_ahead.update({(True, 3): second, (True, 1): middle, (True, 2): middle, (True, 0): last})
         outer, inner = arrival(), arrival()
         self.far = {0: outer, 3: outer, 1: inner, 2: inner}
-        self.far_crossed, self.far_edges = arrival(), arrival()
+        self.far_crossed, self.far_middle, self.far_edges = (arrival() for _ in range(3))
 
     def k(self, offset, other):
         low = 1 - self.low if other else self.low
@@ -82,7 +82,10 @@
         span = (CHUNKS[c][0], min(CHUNKS[c][1], self.low_edge[0]))
         if span[0] == span[1]:
             return
-        arrival = self.far_crossed if c in self.crossed else self.far_edges
+        if c in self.crossed:
+            arrival = self.far_crossed
+        else:
+            arrival = self.far_edges if c == 3 else self.far_middle
         self.move(2, False, span, target, arrival)
 
 
@@ -188,7 +191,7 @@
     both = (rows, cols)
     crossed = [Arrival() for _ in CHUNKS]
     turned = [Arrival() for _ in CHUNKS]
-    shared = [Arrival() for _ in range(6)]
+    shared = [Arrival() for _ in range(7)]
 
     def share(stage, offset, other, span):
         cols.move(offset, other, span, sibling, shared[stage])
@@ -361,9 +364,12 @@
                 ((1,), (1,), (near_first, near_last)),
             ),
         )
+        if offset == 1:
+            cols.far_middle.wait()
+            share(6, 2, True, (TAIL, 2 * TAIL))
 
     cols.far_edges.wait()
-    share(4, 2, True, far_cols_last)
+    share(4, 2, True, (2 * TAIL, ROWS))
     rows.from_behind[True, 0].wait()
     stage_of(
         rows,
@@ -371,6 +377,7 @@
         ((1,), (0, 1), (near_last, WHOLE)),
         ((1,), (2,), (near_last, far_cols_first)),
     )
+    shared[6].wait()
     shared[4].wait()
     product(cols.k(2, True), WHOLE, far_cols_last)
 

time: 79 us -> 79 us (level)
  no operation moved by 1% of the time
where the time goes in v11:
time: 79 us; the launch traced here: 78.8 us
  Pallas kernels  77.8 us (98%)
  local copies, waits for them, and re-layouts  1.02 us (1%)
    pallas_call x1, Pallas kernels, shards(): pl.pallas_call(kernel, out_shape=jax.ShapeDtypeStruct((ROWS, COLS), jnp.f...  77.8 us

profile of v11, /device:TPU:1, one launch (start us, length us, event | category | flops | bytes accessed | tf_op | source)
XLA Modules:
  0.0 78.8 jit_solution(344768604661638409)
XLA Ops:
  0.0 77.8 %commutator.1 = f32[384,768]{1,0:T(8,128)S(1)} custom-call(bf16[384,768]{1,0:T(8,128)(2,1)} %ham.1, bf16[384,768]{1,0:T(8,128)(2,1)} %den.1, s32[6,12]{1,0:T(8,128)} %h_pat.1, s32[6,12]{1,0:T(8,128)} %p_pat.1, s32[6,12]{1,0:T(8,128)} %keep.1), custom_call_target="tpu_custom_call" | custom-call | tf_op jit(solution)/shard_map/commutator/pallas_call | solution.py:394
  77.8 1.0 %copy.7 = f32[384,768]{1,0:T(8,128)} copy(f32[384,768]{1,0:T(8,128)S(1)} %commutator.1) | data formatting | bytes 2359296
